TPU v7x, 128 devices: a whole 4x4x4 slice. The times are simulated.
128 devices in a mesh: seq: 32 (over y, z, core), tile: 4 (over x).
Axes of the slice: x: 4, y: 4, z: 4, core: 2. Of those that a mesh axis runs over, the one named last changes fastest.
Arguments:
- tile_features: bfloat16 [16384, 1536], P(('seq', 'tile')), may hold values from -36 to 36
- gate_weight: bfloat16 [1536, 2048], replicated, may hold values from -0.15625 to 0.15625
- up_weight: bfloat16 [1536, 2048], replicated, may hold values from -0.15625 to 0.15625
- down_weight: bfloat16 [2048, 1536], replicated, may hold values from -0.125 to 0.125
- input_projection_weight: bfloat16 [1536, 768], replicated
- query_key_value_weight: bfloat16 [768, 2304], replicated
- positions: int32 [16384], replicated, may hold values from 0 to 16383, as said below
- dilation_shift: int32 [2, 16], replicated, may hold values from 0 to 15, as said below
- slide_output_gradient: bfloat16 [16384, 768], P('seq', 'tile'), may hold values from -6 to 6
Outputs:
- slide_out: bfloat16 [16384, 768], P('seq', 'tile')
- tile_grad: bfloat16 [16384, 1536], P(('seq', 'tile'))
Inputs may be any that keep to these rules, and one draw needn't show every extreme that they name: Each slide position belongs to exactly one tile. Of one device's tiles at most 8 fall in one block of 512 positions, and in every draw some device reaches 8. `dilation_shift`: row 0 lies below 4, row 1 below 16.
All inputs are finite; a program needn't handle non-finite values.
Results may differ from a plain program's by a relative error of at most 0.039.
Values may be sent and summed in bfloat16 or wider, within the bound.
No kernel may reach another device: no remote copies, remote signals or barrier semaphores. Data moves between devices by JAX's collectives and lax.ppermute only.
A program may use at most 128 MiB of HBM per device.

v0:
```python
import jax
import jax.numpy as jnp
from jax import lax
from jax.experimental import pallas as pl
from jax.experimental.pallas import tpu as pltpu
from jax.sharding import PartitionSpec as P

HEADS = 16
HD = 48
EPSILON = 1e-06
SOFT_CAP = 50.0
SCALE = HD**-0.5
LOG2_E = 1.4426950408889634
BLK = 512
SLOTS = 8
BF = jnp.bfloat16
F32 = jnp.float32
I32 = jnp.int32

NN = (((1,), (0,)), ((), ()))
NT = (((1,), (1,)), ((), ()))
TN = (((0,), (0,)), ((), ()))


def mm(a, b, dims=NN):
    return lax.dot_general(a, b, dims, preferred_element_type=F32)


def iota(shape, dim):
    return lax.broadcasted_iota(I32, shape, dim)


def class_order(row):
    return (row & 3) * 128 + ((row >> 2) & 3) * 32 + (row >> 4)


def order_matrix():
    return jnp.where(class_order(iota((BLK, BLK), 0)) == iota((BLK, BLK), 1), 1.0, 0.0).astype(BF)


def normalize(values):
    centred = values - jnp.mean(values, axis=-1, keepdims=True)
    inv_std = lax.rsqrt(jnp.mean(centred * centred, axis=-1, keepdims=True) + EPSILON)
    return (centred * inv_std, inv_std)


def norm_back(normed, inv_std, grads):
    mean_grad = jnp.mean(grads, axis=-1, keepdims=True)
    mean_cross = jnp.mean(grads * normed, axis=-1, keepdims=True)
    return (grads - mean_grad - normed * mean_cross) * inv_std


def call(kernel, outs, scratch=(), n_smem=0, n_any=0, n_hbm=0, n_hbm_out=0, limit=4):
    def run(*args):
        n_vmem = len(args) - n_smem - n_any - n_hbm
        specs = [pl.BlockSpec(memory_space=pltpu.SMEM)] * n_smem
        specs += [pl.BlockSpec(memory_space=pltpu.VMEM)] * n_vmem
        specs += [pl.BlockSpec(memory_space=pl.ANY)] * n_any
        specs += [pl.BlockSpec(memory_space=pltpu.HBM)] * n_hbm
        out_specs = [pl.BlockSpec(memory_space=pltpu.HBM)] * n_hbm_out
        out_specs += [pl.BlockSpec(memory_space=pltpu.VMEM)] * (len(outs) - n_hbm_out)
        shapes = [pltpu.HBM(shape, kind) for shape, kind in outs[:n_hbm_out]]
        shapes += [jax.ShapeDtypeStruct(shape, kind) for shape, kind in outs[n_hbm_out:]]
        cut = len(args) - n_hbm
        held = [pltpu.with_memory_space_constraint(x, pltpu.HBM) for x in args[cut:]]
        return pl.pallas_call(
            kernel,
            out_shape=shapes,
            in_specs=specs,
            out_specs=out_specs,
            scratch_shapes=list(scratch),
            compiler_params=pltpu.CompilerParams(vmem_limit_bytes=limit * 1024 * 1024),
        )(*args[:cut], *held)

    return run


def started(copies):
    for copy in copies:
        copy.start()
    return copies


def finish(copies):
    for copy in copies:
        copy.wait()


def order_kernel(grad_ref, g0_ref, g1_ref, g2_ref, g3_ref, tmp_ref):
    j = lax.axis_index("seq") & 3
    tmp_ref[...] = mm(grad_ref[...], order_matrix()).astype(BF)
    for d, out_ref in enumerate((g0_ref, g1_ref, g2_ref, g3_ref)):
        out_ref[...] = tmp_ref[pl.ds(pl.multiple_of((j ^ d) * HD, 16), HD), :]


def offsets(shift_ref):
    head = 4 * lax.axis_index("tile") + (lax.axis_index("seq") & 3)
    o1 = shift_ref[0, head]
    o2 = shift_ref[1, head]
    return (o1 * 128, (o2 & 3) * 128, o2 >> 2)


def table_kernel(pos_ref, row_ref, col_ref):
    s = lax.axis_index("seq")
    pos = pos_ref[...].T
    n = pos.shape[0]
    block = pos >> 9
    seat = class_order(pos & (BLK - 1)) + 1
    lower = jnp.where(iota((n, n), 1) < iota((n, n), 0), 1.0, 0.0).astype(BF)
    high, low = [], []
    for d in range(4):
        owned = block == (s ^ d)
        rank = mm(lower, jnp.where(owned, 1.0, 0.0).astype(BF)).astype(I32)
        held = jnp.where(owned, seat, 0)
        for k in range(SLOTS):
            found = jnp.sum(jnp.where(rank == k, held, 0), axis=0, keepdims=True)
            high.append(found >> 4)
            low.append(found & 15)
    digits = jnp.concatenate(high + low, axis=0).astype(F32).astype(BF)
    lanes = n * SLOTS
    spread = jnp.where(iota((n, lanes), 0) == iota((n, lanes), 1) >> 3, 1.0, 0.0).astype(BF)
    wide = mm(digits, spread)
    wide = 16.0 * wide[0:32] + wide[32:64]
    own = iota((8, lanes), 0) == (iota((8, lanes), 1) & 7)
    rows = [
        jnp.sum(jnp.where(own, wide[8 * d : 8 * d + 8], 0.0), axis=0, keepdims=True)
        for d in range(4)
    ]
    table = jnp.concatenate(rows + rows, axis=0) - 1.0
    row_ref[...] = table.astype(I32)
    col_ref[...] = table.T.astype(I32)


def forward_mlp_kernel(
    feat_hbm,
    pos_hbm,
    gate_hbm,
    up_hbm,
    down_hbm,
    proj_hbm,
    qkvw_hbm,
    out_hbm,
    x_hbm,
    a1_hbm,
    a2_hbm,
    feat_ref,
    pos_ref,
    wg_ref,
    wu_ref,
    wd_ref,
    wp_ref,
    wq_ref,
    x_ref,
    a1_ref,
    a2_ref,
    heads_ref,
    picker_ref,
    tmp_ref,
    sems,
    out_sems,
):
    ff = gate_hbm.shape[1]
    width = HEADS * HD
    step = 512
    chunks = ff // step
    first = started(
        [
            pltpu.make_async_copy(feat_hbm, feat_ref, sems.at[3 * chunks]),
            pltpu.make_async_copy(pos_hbm, pos_ref, sems.at[3 * chunks + 1]),
        ]
    )
    waits = []
    for c in range(chunks):
        at = pl.ds(c * step, step)
        waits.append(
            started(
                [
                    pltpu.make_async_copy(gate_hbm.at[:, at], wg_ref.at[:, at], sems.at[3 * c]),
                    pltpu.make_async_copy(up_hbm.at[:, at], wu_ref.at[:, at], sems.at[3 * c + 1]),
                    pltpu.make_async_copy(down_hbm.at[at, :], wd_ref.at[at, :], sems.at[3 * c + 2]),
                ]
            )
        )
    last = started(
        [
            pltpu.make_async_copy(proj_hbm, wp_ref, sems.at[3 * chunks + 2]),
        ]
        + [
            pltpu.make_async_copy(qkvw_hbm.at[:, at], wq_ref.at[:, at], sems.at[3 * chunks + 3 + i])
            for i, at in enumerate(pl.ds(width * part, width) for part in range(3))
        ]
    )
    finish(first)

    me = lax.axis_index("seq") * 4 + lax.axis_index("tile")
    brow = pos_ref[pl.ds(me, 1), :] >> 9
    n = brow.shape[1]
    bcol = jnp.broadcast_to(brow, (n, n)).T
    before = iota((n, n), 0) < iota((n, n), 1)
    rank = jnp.sum(jnp.where((bcol == brow) & before, 1, 0), axis=0, keepdims=True)
    code = brow * SLOTS + rank
    code = jnp.concatenate([code, code + 4096], axis=1)
    seat = iota((BLK, 2 * n), 0)
    want = (((seat >> 4) & 7) * 4 + (seat >> 7)) * SLOTS + (seat & 7) + 4096 * ((seat >> 3) & 1)
    picker_ref[...] = jnp.where(code == want, 1.0, 0.0).astype(BF)

    feats = feat_ref[...].astype(F32)
    normed = normalize(feats)[0].astype(BF)
    total = feats
    outs = []
    for c in range(chunks):
        at = slice(c * step, c * step + step)
        waits[c][0].wait()
        gate = mm(normed, wg_ref[:, at])
        waits[c][1].wait()
        up = mm(normed, wu_ref[:, at])
        sig = jax.nn.sigmoid(gate)
        silu = gate * sig
        hidden = (silu * up).astype(BF)
        a1_ref[:, at] = (up * (sig + silu * (1.0 - sig))).astype(BF)
        a2_ref[:, at] = silu.astype(BF)
        waits[c][2].wait()
        total = total + mm(hidden, wd_ref[at, :])
    outs += started(
        [
            pltpu.make_async_copy(a1_ref, a1_hbm, out_sems.at[0]),
            pltpu.make_async_copy(a2_ref, a2_hbm, out_sems.at[1]),
        ]
    )
    last[0].wait()
    x = mm(total.astype(BF), wp_ref[...]).astype(BF)
    x_ref[...] = x
    outs += started([pltpu.make_async_copy(x_ref, x_hbm, out_sems.at[2])])
    slide_norm = normalize(x.astype(F32))[0].astype(BF)

    def deal(values, part):
        for h in range(HEADS):
            t, j = h // 4, h % 4
            heads_ref[2 * j + t // 2, n * (t % 2) : n * (t % 2) + n, HD * part : HD * part + HD] = (
                values[:, h * HD : h * HD + HD]
            )

    deal(x, 3)
    for part in range(3):
        last[1 + part].wait()
        at = slice(width * part, width * part + width)
        deal(mm(slide_norm, wq_ref[:, at]).astype(BF), part)
    for pair in range(HEADS // 2):
        j = pair // 2
        rows = mm(picker_ref[...], heads_ref[pair]).astype(BF)
        at = slice(16 * pair, 16 * pair + 16)
        for block in range(4):
            lane = (j ^ block) * 192
            tmp_ref[:, at, lane : lane + 192] = rows[128 * block : 128 * block + 128].reshape(
                8, 16, 192
            )
        outs += started(
            [
                pltpu.make_async_copy(
                    tmp_ref.at[:, at, :], out_hbm.at[:, at, :], out_sems.at[3 + pair]
                )
            ]
        )
    finish(outs)


BAND = 256


def band(i):
    return pl.ds(pl.multiple_of(i * BAND, BAND), BAND)


def turn_kernel(
    gate_hbm, up_hbm, _after_hbm, gatet_hbm, upt_hbm, in_ref, out_ref, sems, out_sems
):
    count = gate_hbm.shape[0] // BAND
    given, made = (gate_hbm, up_hbm), (gatet_hbm, upt_hbm)

    def load(which, i):
        return pltpu.make_async_copy(
            given[which].at[band(i), :], in_ref.at[which, band(i), :], sems.at[which, i]
        )

    def store(which, i):
        return pltpu.make_async_copy(
            out_ref.at[which, :, band(i)], made[which].at[:, band(i)], out_sems.at[which, i]
        )

    for which in range(2):
        for i in range(count):
            load(which, i).start()
    for which in range(2):

        def step(i, carry):
            load(which, i).wait()
            out_ref[which, :, band(i)] = in_ref[which, band(i), :].T
            store(which, i).start()
            return carry

        lax.fori_loop(0, count, step, 0)
    for which in range(2):
        for i in range(count):
            store(which, i).wait()


def fold_kernel(
    down_hbm,
    proj_hbm,
    qkvw_hbm,
    _after_hbm,
    fold_hbm,
    projt_hbm,
    qkvt_hbm,
    wd_ref,
    wp_ref,
    wq_ref,
    fold_ref,
    projt_ref,
    qkvt_ref,
    sems,
    out_sems,
):
    count = down_hbm.shape[0] // BAND
    loads = started(
        [
            pltpu.make_async_copy(qkvw_hbm, wq_ref, sems.at[count]),
            pltpu.make_async_copy(proj_hbm, wp_ref, sems.at[count + 1]),
        ]
    )

    def load(i):
        return pltpu.make_async_copy(down_hbm.at[band(i), :], wd_ref.at[band(i), :], sems.at[i])

    def store(i):
        return pltpu.make_async_copy(
            fold_ref.at[:, band(i)], fold_hbm.at[:, band(i)], out_sems.at[i]
        )

    def turn(from_ref, to_ref):
        def step(i, carry):
            to_ref[:, band(i)] = from_ref[band(i), :].T
            return carry

        lax.fori_loop(0, from_ref.shape[0] // BAND, step, 0)

    for i in range(count):
        load(i).start()
    loads[0].wait()
    turn(wq_ref, qkvt_ref)
    outs = started([pltpu.make_async_copy(qkvt_ref, qkvt_hbm, out_sems.at[count])])
    loads[1].wait()
    turn(wp_ref, projt_ref)
    outs += started([pltpu.make_async_copy(projt_ref, projt_hbm, out_sems.at[count + 1])])

    def step(i, carry):
        load(i).wait()
        fold_ref[:, band(i)] = mm(wd_ref[band(i), :], wp_ref[...]).astype(BF).T
        store(i).start()
        return carry

    lax.fori_loop(0, count, step, 0)
    for i in range(count):
        store(i).wait()
    finish(outs)


def backward_mlp_kernel(
    ret_ref,
    s0_any,
    s1_any,
    s2_any,
    s3_any,
    pos_hbm,
    feat_hbm,
    x_hbm,
    a1_hbm,
    a2_hbm,
    gate_hbm,
    up_hbm,
    fold_hbm,
    proj_hbm,
    qkvw_hbm,
    out_ref,
    slide_ref,
    pos_ref,
    feat_ref,
    x_ref,
    a1_ref,
    a2_ref,
    wg_ref,
    wu_ref,
    fold_ref,
    wp_ref,
    wq_ref,
    dqkv_ref,
    grad_ref,
    tmp_ref,
    sems,
):
    ff = gate_hbm.shape[0]
    cuts = [(at, 512) for at in range(0, ff - 512, 512)] + [(ff - 512, 256), (ff - 256, 256)]
    chunks = len(cuts)
    pairs = (
        (pos_hbm, pos_ref),
        (x_hbm, x_ref),
        (qkvw_hbm, wq_ref),
        (proj_hbm, wp_ref),
        (a1_hbm, a1_ref),
        (a2_hbm, a2_ref),
        (feat_hbm, feat_ref),
    )
    first = started(
        [
            pltpu.make_async_copy(here, there, sems.at[3 * chunks + i])
            for i, (here, there) in enumerate(pairs)
        ]
    )
    waits = []
    for c, (start, size) in enumerate(cuts):
        at = pl.ds(start, size)
        waits.append(
            started(
                [
                    pltpu.make_async_copy(fold_hbm.at[:, at], fold_ref.at[:, at], sems.at[3 * c]),
                    pltpu.make_async_copy(gate_hbm.at[at, :], wg_ref.at[at, :], sems.at[3 * c + 1]),
                    pltpu.make_async_copy(up_hbm.at[at, :], wu_ref.at[at, :], sems.at[3 * c + 2]),
                ]
            )
        )
    j = lax.axis_index("seq") & 3
    pieces = started(
        [
            pltpu.make_async_copy(
                so,
                tmp_ref.at[pl.ds(pl.multiple_of((j ^ d) * HD, 16), HD), :],
                sems.at[3 * chunks + len(pairs) + d],
            )
            for d, so in enumerate((s0_any, s1_any, s2_any, s3_any))
        ]
    )
    first[0].wait()
    me = lax.axis_index("seq") * 4 + lax.axis_index("tile")
    brow = pos_ref[pl.ds(me, 1), :] >> 9
    n = brow.shape[1]
    bcol = jnp.broadcast_to(brow, (n, n)).T
    before = iota((n, n), 1) < iota((n, n), 0)
    rank = jnp.sum(jnp.where((bcol == brow) & before, 1, 0), axis=1, keepdims=True)
    code = bcol[:, 0:1] * SLOTS + rank
    code = jnp.concatenate([code, code + 4096], axis=0)
    seat = iota((2 * n, BLK), 1)
    want = (((seat >> 4) & 7) * 4 + (seat >> 7)) * SLOTS + (seat & 7) + 4096 * ((seat >> 3) & 1)
    picker = jnp.where(code == want, 1.0, 0.0).astype(BF)
    width = HEADS * HD
    for pair in range(HEADS // 2):
        j, t = pair // 2, 2 * (pair % 2)
        tile = ret_ref[:, 16 * pair : 16 * pair + 16, :].reshape(128, 768)
        stacked = jnp.concatenate(
            [tile[:, (j ^ b) * 192 : (j ^ b) * 192 + 192] for b in range(4)], axis=0
        )
        got = mm(picker, stacked).astype(BF)
        for tp in range(2):
            h = 4 * (t + tp) + j
            mine = got[n * tp : n * tp + n]
            for part in range(3):
                dqkv_ref[:, part * width + h * HD : part * width + h * HD + HD] = mine[
                    :, HD * part : HD * part + HD
                ]
            grad_ref[:, h * HD : h * HD + HD] = mine[:, 144:192]
    first[1].wait()
    slide_norm, slide_inv = normalize(x_ref[...].astype(F32))
    first[2].wait()
    dnorm = mm(dqkv_ref[...], wq_ref[...])
    dslide = (grad_ref[...].astype(F32) + norm_back(slide_norm, slide_inv, dnorm)).astype(BF)
    first[3].wait()
    dembed = mm(dslide, wp_ref[...]).astype(BF)
    finish(first[4:])
    normed, inv = normalize(feat_ref[...].astype(F32))
    finish(pieces)
    slide_ref[...] = mm(tmp_ref[...], order_matrix(), NT).astype(BF)
    dfeat = jnp.zeros(feat_ref.shape, F32)
    for c, (start, size) in enumerate(cuts):
        at = slice(start, start + size)
        waits[c][0].wait()
        dhidden = mm(dslide, fold_ref[:, at])
        dgate = (dhidden * a1_ref[:, at].astype(F32)).astype(BF)
        dup = (dhidden * a2_ref[:, at].astype(F32)).astype(BF)
        waits[c][1].wait()
        dfeat = dfeat + mm(dgate, wg_ref[at, :])
        waits[c][2].wait()
        dfeat = dfeat + mm(dup, wu_ref[at, :])
    out_ref[...] = (dembed.astype(F32) + norm_back(normed, inv, dfeat)).astype(BF)


def place_kernel(shift_ref, recv_ref, tab_ref, _after_hbm, y_ref, yt_ref, y2_ref):
    _, base, part = offsets(shift_ref)
    o2 = pl.multiple_of(base + 32 * part, 32)
    for d in range(4):
        tab = tab_ref[d : d + 1, :]
        onehot = jnp.where(iota((BLK, tab.shape[1]), 0) == tab, 1.0, 0.0).astype(BF)
        y = mm(onehot, recv_ref[:, 192 * d : 192 * d + 192])
        y = y.astype(BF)
        y_ref[d] = y
        yt_ref[d] = y.T
        y2_ref[32 * d : 32 * d + 32, :] = y_ref[d, pl.ds(o2, 32), :]


def score_rows(keys, queries_t, e_store, m_store):
    count, width = keys.shape[0], queries_t.shape[1]
    total = jnp.zeros((8, width), F32)
    step = 128
    for c in range(0, count, step):
        t = jnp.tanh(mm(keys[c : c + step], queries_t) * (SCALE / SOFT_CAP))
        e = jnp.exp2((SOFT_CAP * LOG2_E) * t)
        total = total + jnp.sum(e.reshape(step // 8, 8, width), axis=0)
        e_store(c, step, e.astype(BF))
        m_store(c, step, (e - e * (t * t)).astype(BF))
    return jnp.sum(total, axis=0, keepdims=True)


def forward_kernel(shift_ref, y_ref, yt_ref, e0_ref, m0_ref, e1_ref, m1_ref, u_ref, l_ref):
    o1 = pl.multiple_of(offsets(shift_ref)[0], 128)

    def block(d):
        def e_store(c, n, v):
            e0_ref[d, c : c + n, :] = v

        def m_store(c, n, v):
            m0_ref[d, c : c + n, :] = v

        l_ref[d] = score_rows(y_ref[d, :, 48:96], yt_ref[d, 0:48, :], e_store, m_store)
        u_ref[d] = mm(yt_ref[d, 96:144, :], e0_ref[d])

    for d in range(4):
        block(d)

    def e_store(c, n, v):
        e1_ref[c : c + n, :] = v

    def m_store(c, n, v):
        m1_ref[c : c + n, :] = v

    keys = jnp.concatenate([y_ref[d, pl.ds(o1, 128), 48:96] for d in range(4)], axis=0)
    queries = jnp.concatenate([yt_ref[d, 0:48, pl.ds(o1, 128)] for d in range(4)], axis=1)
    values = jnp.concatenate([yt_ref[d, 96:144, pl.ds(o1, 128)] for d in range(4)], axis=1)
    l1 = score_rows(keys, queries, e_store, m_store)
    u1 = mm(values, e1_ref[...])
    for d in range(4):
        u_ref[d, :, pl.ds(o1, 128)] += u1[:, 128 * d : 128 * d + 128]
        l_ref[d, :, pl.ds(o1, 128)] += l1[:, 128 * d : 128 * d + 128]


def turned(value, shift):
    return pltpu.roll(value, shift & 127, 1)


def wide_kernel(
    shift_ref,
    yt_ref,
    a0_ref,
    a1_ref,
    a2_ref,
    a3_ref,
    u_ref,
    l_ref,
    g0_ref,
    g1_ref,
    g2_ref,
    g3_ref,
    so0_hbm,
    so1_hbm,
    so2_hbm,
    so3_hbm,
    gs_ref,
    ds_ref,
    own_ref,
    send1_ref,
    send2_ref,
    send3_ref,
    dq_ref,
    e2_ref,
    m2_ref,
    usum_ref,
    lsum_ref,
    so_ref,
    so_sems,
):
    outs = []
    _, base, part = offsets(shift_ref)
    base = pl.multiple_of(base, 128)
    y2 = jnp.concatenate([a0_ref[...], a1_ref[...], a2_ref[...], a3_ref[...]], axis=0)
    keys, values = y2[:, 48:96], y2[:, 96:144]
    both_t = y2[:, 48:144].astype(F32).T.astype(BF)
    query_t = a0_ref[:, 0:48].astype(F32).T.astype(BF)

    def e_store(c, n, v):
        e2_ref[c : c + n, :] = v

    def m_store(c, n, v):
        m2_ref[c : c + n, :] = v

    l2 = score_rows(keys, query_t, e_store, m_store)
    u2 = mm(both_t[48:96], e2_ref[...])
    l2w = jnp.broadcast_to(l2, (8, 128))
    lane = iota((1, 128), 1) >> 5
    gs2 = jnp.zeros((48, 128), F32)
    ds2 = jnp.zeros((8, 128), F32)
    for d in range(4):
        here = lane == part
        shift = 32 * (part - d)
        usum_ref[...] = u_ref[d]
        lsum_ref[...] = l_ref[d]
        usum_ref[:, pl.ds(base, 128)] += jnp.where(here, turned(u2, shift), 0.0)
        lsum_ref[:, pl.ds(base, 128)] += jnp.where(here, turned(l2w, shift), 0.0)[0:1]
        inv = 1.0 / lsum_ref[...]
        att = usum_ref[...] * inv
        so_ref[d] = (yt_ref[d, 144:192, :].astype(F32) + att).astype(BF)
        so = (so0_hbm, so1_hbm, so2_hbm, so3_hbm)[d]
        outs += started([pltpu.make_async_copy(so_ref.at[d], so, so_sems.at[d])])
        grad_ref = (g0_ref, g1_ref, g2_ref, g3_ref)[d]
        gs = (grad_ref[...].astype(F32) * inv).astype(BF)
        gs_ref[d] = gs
        ds_ref[d] = jnp.sum(gs.astype(F32) * att, axis=0, keepdims=True)
        gs_wide = gs_ref[d, :, pl.ds(base, 128)].astype(F32)
        ds_wide = jnp.broadcast_to(ds_ref[d, :, pl.ds(base, 128)], (8, 128))
        gs2 = jnp.where(lane == d, turned(gs_wide, -shift), gs2)
        ds2 = jnp.where(lane == d, turned(ds_wide, -shift), ds2)
    gs2 = gs2.astype(BF)
    dp = mm(values, gs2)
    dscore = (m2_ref[...].astype(F32) * (dp - ds2[0:1])).astype(BF)
    dq_ref[...] = mm(both_t[0:48], dscore) * SCALE
    dk = mm(query_t, dscore, NT) * SCALE
    dv = mm(gs2, e2_ref[...], NT)
    dkv = jnp.concatenate([dk, dv], axis=0)
    own_ref[...] = dkv[:, 0:128]
    for e, send_ref in enumerate((send1_ref, send2_ref, send3_ref)):
        send_ref[...] = dkv[:, 128 * e + 128 : 128 * e + 256].astype(BF)
    finish(outs)


def dscores(values, gs, ds, m_load, store):
    dp = mm(values, gs)
    step = 64
    for c in range(0, dp.shape[0], step):
        store(c, step, (m_load(c, step).astype(F32) * (dp[c : c + step] - ds)).astype(BF))


def backward_kernel(
    shift_ref, y_ref, yt_ref, e0_ref, m0_ref, e1_ref, m1_ref, gs_ref, ds_ref, out_ref, tmp_ref
):
    o1 = pl.multiple_of(offsets(shift_ref)[0], 128)

    def store(c, n, v):
        tmp_ref[c : c + n, :] = v

    def block(d):
        gs = gs_ref[d]
        dscores(y_ref[d, :, 96:144], gs, ds_ref[d], lambda c, n: m0_ref[d, c : c + n, :], store)
        dscore = tmp_ref[...]
        out_ref[d, 0:48, :] = mm(yt_ref[d, 48:96, :], dscore) * SCALE
        out_ref[d, 48:96, :] = mm(yt_ref[d, 0:48, :], dscore, NT) * SCALE
        out_ref[d, 96:144, :] = mm(gs, e0_ref[d], NT)

    for d in range(4):
        block(d)
    values = jnp.concatenate([y_ref[d, pl.ds(o1, 128), 96:144] for d in range(4)], axis=0)
    queries = jnp.concatenate([yt_ref[d, 0:48, pl.ds(o1, 128)] for d in range(4)], axis=1)
    keys = jnp.concatenate([yt_ref[d, 48:96, pl.ds(o1, 128)] for d in range(4)], axis=1)
    gs = jnp.concatenate([gs_ref[d, :, pl.ds(o1, 128)] for d in range(4)], axis=1)
    ds = jnp.concatenate([ds_ref[d, :, pl.ds(o1, 128)] for d in range(4)], axis=1)
    dscores(values, gs, ds, lambda c, n: m1_ref[c : c + n, :], store)
    dscore = tmp_ref[...]
    dq = mm(keys, dscore) * SCALE
    dk = mm(queries, dscore, NT) * SCALE
    dv = mm(gs, e1_ref[...], NT)
    dall = jnp.concatenate([dq, dk, dv], axis=0)
    for d in range(4):
        out_ref[d, :, pl.ds(o1, 128)] += dall[:, 128 * d : 128 * d + 128]


def return_kernel(
    shift_ref,
    dall_ref,
    own_ref,
    dq_ref,
    r1_ref,
    r2_ref,
    r3_ref,
    g0_ref,
    g1_ref,
    g2_ref,
    g3_ref,
    tab_ref,
    out_hbm,
    sum_ref,
    out_ref,
    sems,
):
    _, base, part = offsets(shift_ref)
    base = pl.multiple_of(base, 128)
    dkv = (
        own_ref[...]
        + r1_ref[...].astype(F32)
        + r2_ref[...].astype(F32)
        + r3_ref[...].astype(F32)
    )
    extra = jnp.concatenate([dq_ref[...], dkv], axis=0)
    lane = iota((1, 128), 1) >> 5
    rows = tab_ref.shape[0]
    step = rows // 4
    outs, parts = [], []
    for d in range(4):
        grad_ref = (g0_ref, g1_ref, g2_ref, g3_ref)[d]
        sum_ref[...] = dall_ref[d]
        sum_ref[:, pl.ds(base, 128)] += jnp.where(
            lane == part, turned(extra, 32 * (part - d)), 0.0
        )
        parts.append(jnp.concatenate([sum_ref[...].astype(BF), grad_ref[...]], axis=0).T)
    for c in range(4):
        at = slice(step * c, step * c + step)
        for d in range(4):
            onehot = jnp.where(tab_ref[at, d : d + 1] == iota((step, BLK), 1), 1.0, 0.0)
            out_ref[at, 192 * d : 192 * d + 192] = mm(onehot.astype(BF), parts[d]).astype(BF)
        outs += started([pltpu.make_async_copy(out_ref.at[at, :], out_hbm.at[at, :], sems.at[c])])
    finish(outs)


def swap(value, distance, count):
    return lax.ppermute(value, "seq", [(i, i ^ distance) for i in range(count)])


def on_device(
    tile_features,
    gate_weight,
    up_weight,
    down_weight,
    input_projection_weight,
    query_key_value_weight,
    positions,
    dilation_shift,
    slide_output_gradient,
):
    seq_count = lax.axis_size("seq")
    device_count = seq_count * lax.axis_size("tile")
    rows, width = tile_features.shape
    ff = gate_weight.shape[1]
    slide_width = input_projection_weight.shape[1]
    all_pos = positions.reshape(device_count, rows)
    routed = ((8, 16 * SLOTS, slide_width), BF)
    weights = (gate_weight, up_weight, down_weight, input_projection_weight, query_key_value_weight)

    def exchange(block):
        return lax.all_to_all(
            block.reshape(device_count, SLOTS, slide_width),
            ("seq", "tile"),
            split_axis=0,
            concat_axis=0,
            tiled=True,
        ).reshape(device_count * SLOTS, slide_width)

    stored = [
        pltpu.VMEM((width, ff), BF),
        pltpu.VMEM((width, ff), BF),
        pltpu.VMEM((ff, width), BF),
        pltpu.VMEM((width, slide_width), BF),
        pltpu.VMEM((slide_width, 3 * slide_width), BF),
    ]
    dma = pltpu.SemaphoreType.DMA
    outgoing, x, a1, a2 = call(
        forward_mlp_kernel,
        [routed, ((rows, slide_width), BF), ((rows, ff), BF), ((rows, ff), BF)],
        [pltpu.VMEM((rows, width), BF), pltpu.VMEM((device_count, rows), I32)]
        + stored
        + [
            pltpu.VMEM((rows, slide_width), BF),
            pltpu.VMEM((rows, ff), BF),
            pltpu.VMEM((rows, ff), BF),
            pltpu.VMEM((HEADS // 2, 2 * rows, 192), BF),
            pltpu.VMEM((BLK, 2 * rows), BF),
            pltpu.VMEM((8, 16 * SLOTS, slide_width), BF),
            dma((18,)),
            dma((3 + HEADS // 2,)),
        ],
        n_hbm=7,
        n_hbm_out=4,
        limit=48,
    )(tile_features, all_pos, *weights)
    arrived = exchange(outgoing)
    turned_ff = call(
        turn_kernel,
        [((ff, width), BF)] * 2,
        [
            pltpu.VMEM((2, width, ff), BF),
            pltpu.VMEM((2, ff, width), BF),
            dma((2, width // BAND)),
            dma((2, width // BAND)),
        ],
        n_hbm=3,
        n_hbm_out=2,
        limit=32,
    )(gate_weight, up_weight, x)

    grads = call(
        order_kernel,
        [((HD, BLK), BF)] * 4,
        [pltpu.VMEM((192, BLK), BF)],
    )(slide_output_gradient.T)
    grads = [grads[0]] + [swap(grads[d], d, seq_count) for d in range(1, 4)]
    slots = device_count * SLOTS
    table, table_col = call(
        table_kernel,
        [((8, slots), I32), ((slots, 8), I32)],
    )(all_pos)

    y, yt, y2 = call(
        place_kernel,
        [((4, BLK, 192), BF), ((4, 192, BLK), BF), ((128, 192), BF)],
        n_smem=1,
        n_hbm=1,
    )(dilation_shift, arrived, table, turned_ff[0])
    y2_in = [swap(y2, 4 * e, seq_count) for e in range(1, 4)]
    e0, m0, e1, m1, u, l = call(
        forward_kernel,
        [
            ((4, BLK, BLK), BF),
            ((4, BLK, BLK), BF),
            ((BLK, BLK), BF),
            ((BLK, BLK), BF),
            ((4, HD, BLK), F32),
            ((4, 1, BLK), F32),
        ],
        n_smem=1,
    )(dilation_shift, y, yt)
    *parts, gs, ds, own, send1, send2, send3, dq2 = call(
        wide_kernel,
        [((HD, BLK), BF)] * 4
        + [((4, HD, BLK), BF), ((4, 1, BLK), F32), ((96, 128), F32)]
        + [((96, 128), BF)] * 3
        + [((HD, 128), F32)],
        [
            pltpu.VMEM((BLK, 128), BF),
            pltpu.VMEM((BLK, 128), BF),
            pltpu.VMEM((HD, BLK), F32),
            pltpu.VMEM((1, BLK), F32),
            pltpu.VMEM((4, HD, BLK), BF),
            dma((4,)),
        ],
        n_smem=1,
        n_hbm_out=4,
    )(dilation_shift, yt, y2, *y2_in, u, l, *grads)
    back = [swap(send, 4 * e, seq_count) for e, send in ((1, send1), (2, send2), (3, send3))]
    (dall,) = call(
        backward_kernel,
        [((4, 144, BLK), F32)],
        [pltpu.VMEM((BLK, BLK), BF)],
        n_smem=1,
    )(dilation_shift, y, yt, e0, m0, e1, m1, gs, ds)
    (returning,) = call(
        return_kernel,
        [((slots, slide_width), BF)],
        [
            pltpu.VMEM((144, BLK), F32),
            pltpu.VMEM((slots, slide_width), BF),
            dma((4,)),
        ],
        n_smem=1,
        n_hbm_out=1,
        limit=6,
    )(dilation_shift, dall, own, dq2, *back, *grads, table_col)
    returned = exchange(returning)
    folded = call(
        fold_kernel,
        [
            ((slide_width, ff), BF),
            ((slide_width, width), BF),
            ((3 * slide_width, slide_width), BF),
        ],
        stored[2:]
        + [
            pltpu.VMEM((slide_width, ff), BF),
            pltpu.VMEM((slide_width, width), BF),
            pltpu.VMEM((3 * slide_width, slide_width), BF),
            dma((ff // BAND + 2,)),
            dma((ff // BAND + 2,)),
        ],
        n_hbm=4,
        n_hbm_out=3,
        limit=32,
    )(*weights[2:], returning)
    parts = [parts[0]] + [swap(parts[d], d, seq_count) for d in range(1, 4)]

    tile_grad, slide_out = call(
        backward_mlp_kernel,
        [((rows, width), BF), ((192, BLK), BF)],
        [
            pltpu.VMEM((device_count, rows), I32),
            pltpu.VMEM((rows, width), BF),
            pltpu.VMEM((rows, slide_width), BF),
            pltpu.VMEM((rows, ff), BF),
            pltpu.VMEM((rows, ff), BF),
        ]
        + [pltpu.VMEM(w.shape, BF) for w in (*turned_ff, *folded)]
        + [
            pltpu.VMEM((rows, 3 * slide_width), BF),
            pltpu.VMEM((rows, slide_width), BF),
            pltpu.VMEM((192, BLK), BF),
            dma((26,)),
        ],
        n_any=4,
        n_hbm=10,
        limit=48,
    )(
        returned.reshape(8, 16 * SLOTS, slide_width),
        *parts,
        all_pos,
        tile_features,
        x,
        a1,
        a2,
        *turned_ff,
        *folded,
    )
    return (slide_out.T, tile_grad)


def solution(mesh):
    placed = (P(("seq", "tile"), None), P(), P(), P(), P(), P(), P(), P(), P("seq", "tile"))
    return jax.shard_map(
        on_device,
        mesh=mesh,
        in_specs=placed,
        out_specs=(P("seq", "tile"), P(("seq", "tile"), None)),
        check_vma=False,
    )
```

profile of v0, /device:TPU:1, one launch (start us, length us, event | category | flops | bytes accessed | tf_op | source)
XLA Modules:
  0.0 115.0 jit_solution(10658851673915567906)
XLA Ops:
  0.6 11.8 %shard_map.104 = (bf16[8,128,768]{2,1,0:T(8,128)(2,1)}, bf16[128,768]{1,0:T(8,128)(2,1)}, bf16[128,2048]{1,0:T(8,128)(2,1)}, bf16[128,2048]{1,0:T(8,128)(2,1)}) custom-call(bf16[128,1536]{1,0:T(8,128)(2,1)} %feat_hbm.3, s32[128,128]{1,0:T(8,128)} %bitcast.9, bf16[1536,2048]{1,0:T(8,128)(2,1)} %gate_hbm.3, bf16[1536,2048]{1,0:T(8,128)(2,1)} %up_hbm.3, ...), custom_call_target="tpu_custom_call" | custom-call | tf_op jit(solution)/shard_map/pallas_call | solution.py:66
  12.4 0.0 copy-start.1
  12.4 0.0 copy-start
  12.4 11.5 %all-to-all-start = ((bf16[128,8,768]{2,1,0:T(8,128)(2,1)}), bf16[128,8,768]{2,1,0:T(8,128)(2,1)S(1)}, u32[]{:S(2)}, u32[]{:S(2)}) async-start(bf16[128,8,768]{2,1,0:T(8,128)(2,1)} %bitcast.14), calls=%async_computation | async-start | bytes 3145728 | tf_op jit(solution)/shard_map/all_to_all | solution.py:753
  24.0 0.3 shard_map.109
  24.3 1.1 collective-permute-start.3
  25.4 0.8 collective-permute-start.4
  26.2 0.9 collective-permute-start.5
  27.2 0.9 shard_map.105
  28.1 0.0 copy-start.3
  28.1 9.5 %shard_map.106 = (bf16[2048,1536]{1,0:T(8,128)(2,1)}, bf16[2048,1536]{1,0:T(8,128)(2,1)}) custom-call(bf16[1536,2048]{1,0:T(8,128)(2,1)} %gate_hbm.3, bf16[1536,2048]{1,0:T(8,128)(2,1)} %up_hbm.3, bf16[128,768]{1,0:T(8,128)(2,1)} %get-tuple-element.41._after_hbm.x_hbm), custom_call_target="tpu_custom_call" | custom-call | tf_op jit(solution)/shard_map/pallas_call | solution.py:66
  37.6 11.8 %all-to-all-done = bf16[128,8,768]{2,1,0:T(8,128)(2,1)S(1)} async-done(((bf16[128,8,768]{2,1,0:T(8,128)(2,1)}), bf16[128,8,768]{2,1,0:T(8,128)(2,1)S(1)}, u32[]{:S(2)}, u32[]{:S(2)}) %all-to-all-start) | async-done | bytes 1572896 | tf_op jit(solution)/shard_map/all_to_all | solution.py:753
  49.3 1.9 %shard_map.107 = (bf16[4,512,192]{2,1,0:T(8,128)(2,1)S(1)}, bf16[4,192,512]{2,1,0:T(8,128)(2,1)S(1)}, bf16[128,192]{1,0:T(8,128)(2,1)S(1)}) custom-call(s32[2,16]{1,0:T(2,128)S(1)} %copy-done.3, bf16[1024,768]{1,0:T(8,128)(2,1)S(1)} %bitcast.8, s32[8,1024]{1,0:T(8,128)S(1)} %get-tuple-element.40.tab_ref, bf16[2048,1536]{1,0:T(8,128)(2,1)} %get-tuple-element.42._after_hbm.gate_hbm), custom_call_target="tpu_custom_call" | custom-call | tf_op jit(solution)/shard_map/pallas_call | solution.py:66
  51.3 0.1 collective-permute-start.2
  51.3 1.0 collective-permute-start.1
  52.3 3.2 %collective-permute-start = (bf16[128,192]{1,0:T(8,128)(2,1)S(1)}, bf16[128,192]{1,0:T(8,128)(2,1)S(1)}, u32[]{:S(2)}, u32[]{:S(2)}) collective-permute-start(bf16[128,192]{1,0:T(8,128)(2,1)S(1)} %get-tuple-element.49.a0_ref), channel_id=1, source_target_pairs={{0,16},{4,20},{8,24},{12,28},{16,0},{20,4},{24,8},{28,12},{32,48},... | collective-permute-start | bytes 147464 | tf_op jit(solution)/shard_map/ppermute | solution.py:729
  55.5 3.2 %shard_map.108 = (bf16[4,512,512]{2,1,0:T(8,128)(2,1)S(1)}, bf16[4,512,512]{2,1,0:T(8,128)(2,1)S(1)}, bf16[512,512]{1,0:T(8,128)(2,1)S(1)}, bf16[512,512]{1,0:T(...) custom-call(s32[2,16]{1,0:T(2,128)S(1)} %copy-done.3, ...), custom_call_target="tpu_custom_call" | custom-call | tf_op jit(solution)/shard_map/pallas_call | solution.py:66
  58.8 2.0 %shard_map.110 = (bf16[48,512]{1,0:T(8,128)(2,1)}, bf16[48,512]{1,0:T(8,128)(2,1)}, bf16[48,512]{1,0:T(8,128)(2,1)}, bf16[48,512]{1,0:T(8,128)(2,1)}, bf16[4,48,...) custom-call(s32[2,16]{1,0:T(2,128)S(1)} %copy-done.3, ...), custom_call_target="tpu_custom_call" | custom-call | tf_op jit(solution)/shard_map/pallas_call | solution.py:66
  60.8 1.4 %collective-permute-start.6 = (bf16[96,128]{1,0:T(8,128)(2,1)S(1)}, bf16[96,128]{1,0:T(8,128)(2,1)S(1)}, u32[]{:S(2)}, u32[]{:S(2)}) collective-permute-start(bf16[96,128]{1,0:T(8,128)(2,1)S(1)} %get-tuple-element.60), channel_id=1, source_target_pairs={{0,16},{4,20},{8,24},{12,28},{16,0},{20,4},{24,8},{28,12},{32,48},... | collective-permute-start | bytes 73736 | tf_op jit(solution)/shard_map/ppermute | solution.py:729
  62.2 0.4 collective-permute-start.7
  62.5 2.5 %collective-permute-start.8 = (bf16[96,128]{1,0:T(8,128)(2,1)S(1)}, bf16[96,128]{1,0:T(8,128)(2,1)S(1)}, u32[]{:S(2)}, u32[]{:S(2)}) collective-permute-start(bf16[96,128]{1,0:T(8,128)(2,1)S(1)} %get-tuple-element.62), channel_id=1, source_target_pairs={{0,48},{4,52},{8,56},{12,60},{16,32},{20,36},{24,40},{28,44},{32,1... | collective-permute-start | bytes 73736 | tf_op jit(solution)/shard_map/ppermute | solution.py:729
  65.0 3.7 %shard_map.111.dall_ref = f32[4,144,512]{2,1,0:T(8,128)S(1)} custom-call(s32[2,16]{1,0:T(2,128)S(1)} %copy-done.3, bf16[4,512,192]{2,1,0:T(8,128)(2,1)S(1)} %get-tuple-element.43.y_ref, bf16[4,192,512]{2,1,0:T(8,128)(2,1)S(1)} %get-tuple-element.44.yt_ref, bf16[4,512,512]{2,1,0:T(8,128)(2,1)S(1)} %get-tuple-element.45.e0_ref, ...), custom_call_target="tpu_custom_call" | custom-call | tf_op jit(solution)/shard_map/pallas_call | solution.py:66
  68.8 3.0 %shard_map.112._after_hbm = bf16[1024,768]{1,0:T(8,128)(2,1)} custom-call(s32[2,16]{1,0:T(2,128)S(1)} %copy-done.3, f32[4,144,512]{2,1,0:T(8,128)S(1)} %shard_map.111.dall_ref, f32[96,128]{1,0:T(8,128)S(1)} %get-tuple-element.58.own_ref, f32[48,128]{1,0:T(8,128)S(1)} %get-tuple-element.59.dq_ref, bf16[96,128]{1,0:T(8,128)(2,1)S(1)} %collective-permute-done.6.r1_ref, ...), custom_call_target="tpu_custom_call" | custom-call | tf_op jit(solution)/shard_map/pallas_call | solution.py:66
  71.8 0.0 copy-start.6
  71.9 6.9 %all-to-all-start.1 = ((bf16[128,8,768]{2,1,0:T(8,128)(2,1)}), bf16[128,8,768]{2,1,0:T(8,128)(2,1)S(1)}, u32[]{:S(2)}, u32[]{:S(2)}) async-start(bf16[128,8,768]{2,1,0:T(8,128)(2,1)} %bitcast.13), calls=%async_computation.1 | async-start | bytes 3145728 | tf_op jit(solution)/shard_map/all_to_all | solution.py:753
  78.7 1.1 collective-permute-start.9
  79.9 0.8 collective-permute-start.10
  80.7 0.9 collective-permute-start.11
  81.6 11.8 %shard_map.113 = (bf16[768,2048]{1,0:T(8,128)(2,1)}, bf16[768,1536]{1,0:T(8,128)(2,1)}, bf16[2304,768]{1,0:T(8,128)(2,1)}) custom-call(bf16[2048,1536]{1,0:T(8,128)(2,1)} %down_hbm.3, bf16[1536,768]{1,0:T(8,128)(2,1)} %proj_hbm.3, bf16[768,2304]{1,0:T(8,128)(2,1)} %qkvw_hbm.3, bf16[1024,768]{1,0:T(8,128)(2,1)} %shard_map.112._after_hbm), custom_call_target="tpu_custom_call" | custom-call | tf_op jit(solution)/shard_map/pallas_call | solution.py:66
  93.5 4.1 %collective-permute-done.11.s3_any = bf16[48,512]{1,0:T(8,128)(2,1)S(1)} collective-permute-done((bf16[48,512]{1,0:T(8,128)(2,1)S(1)}, bf16[48,512]{1,0:T(8,128)(2,1)S(1)}, u32[]{:S(2)}, u32[]{:S(2)}) %collective-permute-start.11) | collective-permute-done | bytes 49184 | tf_op jit(solution)/shard_map/ppermute | solution.py:729
  97.6 6.5 %all-to-all-done.1 = bf16[128,8,768]{2,1,0:T(8,128)(2,1)S(1)} async-done(((bf16[128,8,768]{2,1,0:T(8,128)(2,1)}), bf16[128,8,768]{2,1,0:T(8,128)(2,1)S(1)}, u32[]{:S(2)}, u32[]{:S(2)}) %all-to-all-start.1) | async-done | bytes 1572896 | tf_op jit(solution)/shard_map/all_to_all | solution.py:753
  104.1 10.7 %shard_map.114 = (bf16[128,1536]{1,0:T(8,128)(2,1)}, bf16[192,512]{1,0:T(8,128)(2,1)}) custom-call(bf16[8,128,768]{2,1,0:T(8,128)(2,1)S(1)} %bitcast.7, bf16[48,512]{1,0:T(8,128)(2,1)S(1)} %copy-done.2, bf16[48,512]{1,0:T(8,128)(2,1)S(1)} %collective-permute-done.9.s1_any, bf16[48,512]{1,0:T(8,128)(2,1)S(1)} %collective-permute-done.10.s2_any, ...), custom_call_target="tpu_custom_call" | custom-call | tf_op jit(solution)/shard_map/pallas_call | solution.py:66
  (21 shorter events, 0.0 us)
Async XLA Ops:
  12.4 11.5 %copy-start.1 = (bf16[512,192]{0,1:T(8,128)(2,1)S(1)}, bf16[512,192]{0,1:T(8,128)(2,1)}, u32[]{:S(2)}) copy-start(bf16[512,192]{0,1:T(8,128)(2,1)} %param.17) | copy-start | bytes 589828
  12.4 14.7 %copy-start = (s32[16384]{0:T(1024)S(1)}, s32[16384]{0:T(1024)}, u32[]{:S(2)}) copy-start(s32[16384]{0:T(1024)} %param.15) | copy-start | bytes 196612
  12.4 36.9 %all-to-all-start = ((bf16[128,8,768]{2,1,0:T(8,128)(2,1)}), bf16[128,8,768]{2,1,0:T(8,128)(2,1)S(1)}, u32[]{:S(2)}, u32[]{:S(2)}) async-start(bf16[128,8,768]{2,1,0:T(8,128)(2,1)} %bitcast.14), calls=%async_computation | async-start | bytes 3145728 | tf_op jit(solution)/shard_map/all_to_all | solution.py:753
  24.3 28.0 %collective-permute-start.3 = (bf16[48,512]{1,0:T(8,128)(2,1)S(1)}, bf16[48,512]{1,0:T(8,128)(2,1)S(1)}, u32[]{:S(2)}, u32[]{:S(2)}) collective-permute-start(bf16[48,512]{1,0:T(8,128)(2,1)S(1)} %get-tuple-element.53), channel_id=1, source_target_pairs={{0,4},{4,0},{8,12},{12,8},{16,20},{20,16},{24,28},{28,24},{32,36},... | collective-permute-start | bytes 147464 | tf_op jit(solution)/shard_map/ppermute | solution.py:729
  25.4 33.3 %collective-permute-start.4 = (bf16[48,512]{1,0:T(8,128)(2,1)S(1)}, bf16[48,512]{1,0:T(8,128)(2,1)S(1)}, u32[]{:S(2)}, u32[]{:S(2)}) collective-permute-start(bf16[48,512]{1,0:T(8,128)(2,1)S(1)} %get-tuple-element.54), channel_id=1, source_target_pairs={{0,8},{4,12},{8,0},{12,4},{16,24},{20,28},{24,16},{28,20},{32,40},... | collective-permute-start | bytes 147464 | tf_op jit(solution)/shard_map/ppermute | solution.py:729
  26.2 32.5 %collective-permute-start.5 = (bf16[48,512]{1,0:T(8,128)(2,1)S(1)}, bf16[48,512]{1,0:T(8,128)(2,1)S(1)}, u32[]{:S(2)}, u32[]{:S(2)}) collective-permute-start(bf16[48,512]{1,0:T(8,128)(2,1)S(1)} %get-tuple-element.55), channel_id=1, source_target_pairs={{0,12},{4,8},{8,4},{12,0},{16,28},{20,24},{24,20},{28,16},{32,44},... | collective-permute-start | bytes 147464 | tf_op jit(solution)/shard_map/ppermute | solution.py:729
  28.1 21.2 %copy-start.3 = (s32[2,16]{1,0:T(2,128)S(1)}, s32[2,16]{1,0:T(2,128)}, u32[]{:S(2)}) copy-start(s32[2,16]{1,0:T(2,128)} %shift_ref.9) | copy-start | bytes 388
  51.3 7.5 %collective-permute-start.2 = (bf16[128,192]{1,0:T(8,128)(2,1)S(1)}, bf16[128,192]{1,0:T(8,128)(2,1)S(1)}, u32[]{:S(2)}, u32[]{:S(2)}) collective-permute-start(bf16[128,192]{1,0:T(8,128)(2,1)S(1)} %get-tuple-element.49.a0_ref), channel_id=1, source_target_pairs={{0,48},{4,52},{8,56},{12,60},{16,32},{20,36},{24,40},{28,44},{32,1... | collective-permute-start | bytes 147464 | tf_op jit(solution)/shard_map/ppermute | solution.py:729
  51.3 7.4 %collective-permute-start.1 = (bf16[128,192]{1,0:T(8,128)(2,1)S(1)}, bf16[128,192]{1,0:T(8,128)(2,1)S(1)}, u32[]{:S(2)}, u32[]{:S(2)}) collective-permute-start(bf16[128,192]{1,0:T(8,128)(2,1)S(1)} %get-tuple-element.49.a0_ref), channel_id=1, source_target_pairs={{0,32},{4,36},{8,40},{12,44},{16,48},{20,52},{24,56},{28,60},{32,0... | collective-permute-start | bytes 147464 | tf_op jit(solution)/shard_map/ppermute | solution.py:729
  52.3 6.4 %collective-permute-start = (bf16[128,192]{1,0:T(8,128)(2,1)S(1)}, bf16[128,192]{1,0:T(8,128)(2,1)S(1)}, u32[]{:S(2)}, u32[]{:S(2)}) collective-permute-start(bf16[128,192]{1,0:T(8,128)(2,1)S(1)} %get-tuple-element.49.a0_ref), channel_id=1, source_target_pairs={{0,16},{4,20},{8,24},{12,28},{16,0},{20,4},{24,8},{28,12},{32,48},... | collective-permute-start | bytes 147464 | tf_op jit(solution)/shard_map/ppermute | solution.py:729
  60.8 8.0 %collective-permute-start.6 = (bf16[96,128]{1,0:T(8,128)(2,1)S(1)}, bf16[96,128]{1,0:T(8,128)(2,1)S(1)}, u32[]{:S(2)}, u32[]{:S(2)}) collective-permute-start(bf16[96,128]{1,0:T(8,128)(2,1)S(1)} %get-tuple-element.60), channel_id=1, source_target_pairs={{0,16},{4,20},{8,24},{12,28},{16,0},{20,4},{24,8},{28,12},{32,48},... | collective-permute-start | bytes 73736 | tf_op jit(solution)/shard_map/ppermute | solution.py:729
  62.2 6.6 %collective-permute-start.7 = (bf16[96,128]{1,0:T(8,128)(2,1)S(1)}, bf16[96,128]{1,0:T(8,128)(2,1)S(1)}, u32[]{:S(2)}, u32[]{:S(2)}) collective-permute-start(bf16[96,128]{1,0:T(8,128)(2,1)S(1)} %get-tuple-element.61), channel_id=1, source_target_pairs={{0,32},{4,36},{8,40},{12,44},{16,48},{20,52},{24,56},{28,60},{32,0... | collective-permute-start | bytes 73736 | tf_op jit(solution)/shard_map/ppermute | solution.py:729
  62.5 6.2 %collective-permute-start.8 = (bf16[96,128]{1,0:T(8,128)(2,1)S(1)}, bf16[96,128]{1,0:T(8,128)(2,1)S(1)}, u32[]{:S(2)}, u32[]{:S(2)}) collective-permute-start(bf16[96,128]{1,0:T(8,128)(2,1)S(1)} %get-tuple-element.62), channel_id=1, source_target_pairs={{0,48},{4,52},{8,56},{12,60},{16,32},{20,36},{24,40},{28,44},{32,1... | collective-permute-start | bytes 73736 | tf_op jit(solution)/shard_map/ppermute | solution.py:729
  71.8 6.9 %copy-start.6 = (bf16[48,512]{1,0:T(8,128)(2,1)S(1)}, bf16[48,512]{1,0:T(8,128)(2,1)}, u32[]{:S(2)}) copy-start(bf16[48,512]{1,0:T(8,128)(2,1)} %get-tuple-element.65) | copy-start | bytes 147460
  71.8 8.0 %copy-start.5 = (bf16[48,512]{1,0:T(8,128)(2,1)S(1)}, bf16[48,512]{1,0:T(8,128)(2,1)}, u32[]{:S(2)}) copy-start(bf16[48,512]{1,0:T(8,128)(2,1)} %get-tuple-element.66) | copy-start | bytes 147460
  71.9 8.8 %copy-start.4 = (bf16[48,512]{1,0:T(8,128)(2,1)S(1)}, bf16[48,512]{1,0:T(8,128)(2,1)}, u32[]{:S(2)}) copy-start(bf16[48,512]{1,0:T(8,128)(2,1)} %get-tuple-element.67) | copy-start | bytes 147460
  71.9 32.2 %all-to-all-start.1 = ((bf16[128,8,768]{2,1,0:T(8,128)(2,1)}), bf16[128,8,768]{2,1,0:T(8,128)(2,1)S(1)}, u32[]{:S(2)}, u32[]{:S(2)}) async-start(bf16[128,8,768]{2,1,0:T(8,128)(2,1)} %bitcast.13), calls=%async_computation.1 | async-start | bytes 3145728 | tf_op jit(solution)/shard_map/all_to_all | solution.py:753
  78.7 14.7 %collective-permute-start.9 = (bf16[48,512]{1,0:T(8,128)(2,1)S(1)}, bf16[48,512]{1,0:T(8,128)(2,1)S(1)}, u32[]{:S(2)}, u32[]{:S(2)}) collective-permute-start(bf16[48,512]{1,0:T(8,128)(2,1)S(1)} %copy-done.6), channel_id=1, source_target_pairs={{0,4},{4,0},{8,12},{12,8},{16,20},{20,16},{24,28},{28,24},{32,36},... | collective-permute-start | bytes 147464 | tf_op jit(solution)/shard_map/ppermute | solution.py:729
  79.9 13.6 %collective-permute-start.10 = (bf16[48,512]{1,0:T(8,128)(2,1)S(1)}, bf16[48,512]{1,0:T(8,128)(2,1)S(1)}, u32[]{:S(2)}, u32[]{:S(2)}) collective-permute-start(bf16[48,512]{1,0:T(8,128)(2,1)S(1)} %copy-done.5), channel_id=1, source_target_pairs={{0,8},{4,12},{8,0},{12,4},{16,24},{20,28},{24,16},{28,20},{32,40},... | collective-permute-start | bytes 147464 | tf_op jit(solution)/shard_map/ppermute | solution.py:729
  80.7 23.4 %copy-start.2 = (bf16[48,512]{1,0:T(8,128)(2,1)S(1)}, bf16[48,512]{1,0:T(8,128)(2,1)}, u32[]{:S(2)}) copy-start(bf16[48,512]{1,0:T(8,128)(2,1)} %get-tuple-element.64.s0_any) | copy-start | bytes 147460
  80.7 16.9 %collective-permute-start.11 = (bf16[48,512]{1,0:T(8,128)(2,1)S(1)}, bf16[48,512]{1,0:T(8,128)(2,1)S(1)}, u32[]{:S(2)}, u32[]{:S(2)}) collective-permute-start(bf16[48,512]{1,0:T(8,128)(2,1)S(1)} %copy-done.4), channel_id=1, source_target_pairs={{0,12},{4,8},{8,4},{12,0},{16,28},{20,24},{24,20},{28,16},{32,44},... | collective-permute-start | bytes 147464 | tf_op jit(solution)/shard_map/ppermute | solution.py:729
where the time goes:
time: 115 us
  Pallas kernels  59 us (51%)
  starting transfers between devices  32.6 us (28%)
  waiting for transfers between devices  22.4 us (19%)
    pallas_call x11, Pallas kernels, run(): pl.pallas_call(kernel, out_shape=shapes, in_specs=specs, out_specs=out_sp...  59 us
    all_to_all x2, starting transfers between devices, exchange(): lax.all_to_all(block.reshape(device_count, SLOTS, slide_width), ('seq', '...  18.4 us
    all_to_all x2, waiting for transfers between devices, exchange(): lax.all_to_all(block.reshape(device_count, SLOTS, slide_width), ('seq', '...  18.2 us
    ppermute x12, starting transfers between devices, swap(): return lax.ppermute(value, 'seq', [(i, i ^ distance) for i in range(count)])  14.2 us
    ppermute x12, waiting for transfers between devices, swap(): return lax.ppermute(value, 'seq', [(i, i ^ distance) for i in range(count)])  4.16 us
  transfers between devices with their start and end apart: 14, of which 3 were waited for; matrix products, arithmetic and copies ran while one was open for 0% of the time, Pallas kernels for 27%

commit v1 on v0

--- a/solution.py
+++ b/solution.py
@@ -50,7 +50,9 @@
     return (grads - mean_grad - normed * mean_cross) * inv_std
 
 
-def call(kernel, outs, scratch=(), n_smem=0, n_any=0, n_hbm=0, n_hbm_out=0, limit=4):
+def call(
+    kernel, outs, scratch=(), n_smem=0, n_any=0, n_hbm=0, n_hbm_out=0, limit=4, aliases=None
+):
     def run(*args):
         n_vmem = len(args) - n_smem - n_any - n_hbm
         specs = [pl.BlockSpec(memory_space=pltpu.SMEM)] * n_smem
@@ -69,6 +71,7 @@
             in_specs=specs,
             out_specs=out_specs,
             scratch_shapes=list(scratch),
+            input_output_aliases=aliases or {},
             compiler_params=pltpu.CompilerParams(vmem_limit_bytes=limit * 1024 * 1024),
         )(*args[:cut], *held)
 
@@ -86,7 +89,7 @@
         copy.wait()
 
 
-def order_kernel(grad_ref, g0_ref, g1_ref, g2_ref, g3_ref, tmp_ref):
+def order_kernel(grad_ref, _after_hbm, g0_ref, g1_ref, g2_ref, g3_ref, tmp_ref):
     j = lax.axis_index("seq") & 3
     tmp_ref[...] = mm(grad_ref[...], order_matrix()).astype(BF)
     for d, out_ref in enumerate((g0_ref, g1_ref, g2_ref, g3_ref)):
@@ -141,8 +144,6 @@
     qkvw_hbm,
     out_hbm,
     x_hbm,
-    a1_hbm,
-    a2_hbm,
     feat_ref,
     pos_ref,
     wg_ref,
@@ -151,8 +152,6 @@
     wp_ref,
     wq_ref,
     x_ref,
-    a1_ref,
-    a2_ref,
     heads_ref,
     picker_ref,
     tmp_ref,
@@ -217,20 +216,12 @@
         sig = jax.nn.sigmoid(gate)
         silu = gate * sig
         hidden = (silu * up).astype(BF)
-        a1_ref[:, at] = (up * (sig + silu * (1.0 - sig))).astype(BF)
-        a2_ref[:, at] = silu.astype(BF)
         waits[c][2].wait()
         total = total + mm(hidden, wd_ref[at, :])
-    outs += started(
-        [
-            pltpu.make_async_copy(a1_ref, a1_hbm, out_sems.at[0]),
-            pltpu.make_async_copy(a2_ref, a2_hbm, out_sems.at[1]),
-        ]
-    )
     last[0].wait()
     x = mm(total.astype(BF), wp_ref[...]).astype(BF)
     x_ref[...] = x
-    outs += started([pltpu.make_async_copy(x_ref, x_hbm, out_sems.at[2])])
+    outs += started([pltpu.make_async_copy(x_ref, x_hbm, out_sems.at[0])])
     slide_norm = normalize(x.astype(F32))[0].astype(BF)
 
     def deal(values, part):
@@ -257,7 +248,7 @@
         outs += started(
             [
                 pltpu.make_async_copy(
-                    tmp_ref.at[:, at, :], out_hbm.at[:, at, :], out_sems.at[3 + pair]
+                    tmp_ref.at[:, at, :], out_hbm.at[:, at, :], out_sems.at[1 + pair]
                 )
             ]
         )
@@ -272,7 +263,22 @@
 
 
 def turn_kernel(
-    gate_hbm, up_hbm, _after_hbm, gatet_hbm, upt_hbm, in_ref, out_ref, sems, out_sems
+    feat_hbm,
+    gate_hbm,
+    up_hbm,
+    _after_hbm,
+    gatet_hbm,
+    upt_hbm,
+    a1_hbm,
+    a2_hbm,
+    feat_ref,
+    in_ref,
+    out_ref,
+    a1_ref,
+    a2_ref,
+    sems,
+    out_sems,
+    own_sems,
 ):
     count = gate_hbm.shape[0] // BAND
     given, made = (gate_hbm, up_hbm), (gatet_hbm, upt_hbm)
@@ -287,9 +293,12 @@
             out_ref.at[which, :, band(i)], made[which].at[:, band(i)], out_sems.at[which, i]
         )
 
+    feats = started([pltpu.make_async_copy(feat_hbm, feat_ref, own_sems.at[0])])
     for which in range(2):
         for i in range(count):
             load(which, i).start()
+    finish(feats)
+    normed = normalize(feat_ref[...].astype(F32))[0].astype(BF)
     for which in range(2):
 
         def step(i, carry):
@@ -299,6 +308,22 @@
             return carry
 
         lax.fori_loop(0, count, step, 0)
+    size = 512
+    for c in range(0, gate_hbm.shape[1], size):
+        at = slice(c, c + size)
+        gate = mm(normed, in_ref[0, :, at])
+        up = mm(normed, in_ref[1, :, at])
+        sig = jax.nn.sigmoid(gate)
+        silu = gate * sig
+        a1_ref[:, at] = (up * (sig + silu * (1.0 - sig))).astype(BF)
+        a2_ref[:, at] = silu.astype(BF)
+    outs = started(
+        [
+            pltpu.make_async_copy(a1_ref, a1_hbm, own_sems.at[1]),
+            pltpu.make_async_copy(a2_ref, a2_hbm, own_sems.at[2]),
+        ]
+    )
+    finish(outs)
     for which in range(2):
         for i in range(count):
             store(which, i).wait()
@@ -309,9 +334,15 @@
     proj_hbm,
     qkvw_hbm,
     _after_hbm,
+    _in1_hbm,
+    _in2_hbm,
+    _in3_hbm,
     fold_hbm,
     projt_hbm,
     qkvt_hbm,
+    _out1_hbm,
+    _out2_hbm,
+    _out3_hbm,
     wd_ref,
     wp_ref,
     wq_ref,
@@ -766,45 +797,48 @@
         pltpu.VMEM((slide_width, 3 * slide_width), BF),
     ]
     dma = pltpu.SemaphoreType.DMA
-    outgoing, x, a1, a2 = call(
+    outgoing, x = call(
         forward_mlp_kernel,
-        [routed, ((rows, slide_width), BF), ((rows, ff), BF), ((rows, ff), BF)],
+        [routed, ((rows, slide_width), BF)],
         [pltpu.VMEM((rows, width), BF), pltpu.VMEM((device_count, rows), I32)]
         + stored
         + [
             pltpu.VMEM((rows, slide_width), BF),
-            pltpu.VMEM((rows, ff), BF),
-            pltpu.VMEM((rows, ff), BF),
             pltpu.VMEM((HEADS // 2, 2 * rows, 192), BF),
             pltpu.VMEM((BLK, 2 * rows), BF),
             pltpu.VMEM((8, 16 * SLOTS, slide_width), BF),
             dma((18,)),
-            dma((3 + HEADS // 2,)),
+            dma((1 + HEADS // 2,)),
         ],
         n_hbm=7,
-        n_hbm_out=4,
+        n_hbm_out=2,
         limit=48,
     )(tile_features, all_pos, *weights)
     arrived = exchange(outgoing)
-    turned_ff = call(
+    *turned_ff, a1, a2 = call(
         turn_kernel,
-        [((ff, width), BF)] * 2,
-        [
+        [((ff, width), BF)] * 2 + [((rows, ff), BF)] * 2,
+        [
+            pltpu.VMEM((rows, width), BF),
             pltpu.VMEM((2, width, ff), BF),
             pltpu.VMEM((2, ff, width), BF),
+            pltpu.VMEM((rows, ff), BF),
+            pltpu.VMEM((rows, ff), BF),
             dma((2, width // BAND)),
             dma((2, width // BAND)),
+            dma((3,)),
         ],
-        n_hbm=3,
-        n_hbm_out=2,
-        limit=32,
-    )(gate_weight, up_weight, x)
+        n_hbm=4,
+        n_hbm_out=4,
+        limit=36,
+    )(tile_features, gate_weight, up_weight, x)
 
     grads = call(
         order_kernel,
         [((HD, BLK), BF)] * 4,
         [pltpu.VMEM((192, BLK), BF)],
-    )(slide_output_gradient.T)
+        n_hbm=1,
+    )(slide_output_gradient.T, turned_ff[0])
     grads = [grads[0]] + [swap(grads[d], d, seq_count) for d in range(1, 4)]
     slots = device_count * SLOTS
     table, table_col = call(
@@ -868,13 +902,14 @@
         limit=6,
     )(dilation_shift, dall, own, dq2, *back, *grads, table_col)
     returned = exchange(returning)
-    folded = call(
+    *folded, part1, part2, part3 = call(
         fold_kernel,
         [
             ((slide_width, ff), BF),
             ((slide_width, width), BF),
             ((3 * slide_width, slide_width), BF),
-        ],
+        ]
+        + [((HD, BLK), BF)] * 3,
         stored[2:]
         + [
             pltpu.VMEM((slide_width, ff), BF),
@@ -883,11 +918,35 @@
             dma((ff // BAND + 2,)),
             dma((ff // BAND + 2,)),
         ],
-        n_hbm=4,
-        n_hbm_out=3,
+        n_hbm=7,
+        n_hbm_out=6,
         limit=32,
-    )(*weights[2:], returning)
-    parts = [parts[0]] + [swap(parts[d], d, seq_count) for d in range(1, 4)]
+        aliases={4: 3, 5: 4, 6: 5},
+    )(*weights[2:], returning, *parts[1:])
+    *folded, part1, part2, part3 = call(
+        fold_kernel,
+        [
+            ((slide_width, ff), BF),
+            ((slide_width, width), BF),
+            ((3 * slide_width, slide_width), BF),
+        ]
+        + [((HD, BLK), BF)] * 3,
+        stored[2:]
+        + [
+            pltpu.VMEM((slide_width, ff), BF),
+            pltpu.VMEM((slide_width, width), BF),
+            pltpu.VMEM((3 * slide_width, slide_width), BF),
+            dma((ff // BAND + 2,)),
+            dma((ff // BAND + 2,)),
+        ],
+        n_hbm=7,
+        n_hbm_out=6,
+        limit=32,
+        aliases={4: 3, 5: 4, 6: 5},
+    )(*weights[2:], returning, *parts[1:])
+    late = enumerate((part1, part2, part3), 1)
+    parts = [parts[0]] + [swap(piece, d, seq_count) for d, piece in late]
+
 
     tile_grad, slide_out = call(
         backward_mlp_kernel,

time: 115 us -> 116 us (level)
  waiting for transfers between devices: 22.4 us -> 20 us
  Pallas kernels: 59 us -> 61.2 us
    all_to_all x2, waiting for transfers between devices: 18.2 us -> 12.6 us  [exchange(): lax.all_to_all(block.reshape(device_count, SLOTS, slide_width), ('seq', '...]
    ppermute x12, waiting for transfers between devices: 4.16 us -> 7.45 us  [swap(): return lax.ppermute(value, 'seq', [(i, i ^ distance) for i in range(count)])]
    pallas_call x11, Pallas kernels: 59 us -> 61.2 us  [run(): pl.pallas_call(kernel, out_shape=shapes, in_specs=specs, out_specs=out_sp...]
  transfers between devices with their start and end apart: 14 -> 14, of which waited for: 3 -> 4; matrix products, arithmetic and copies ran while one was open for 0% -> 0% of each run, Pallas kernels for 27% -> 29%
where the time goes in v1:
time: 116 us
  Pallas kernels  61.2 us (53%)
  starting transfers between devices  33.6 us (29%)
  waiting for transfers between devices  20 us (17%)
    pallas_call x11, Pallas kernels, run(): pl.pallas_call(kernel, out_shape=shapes, in_specs=specs, out_specs=out_sp...  61.2 us
    all_to_all x2, starting transfers between devices, exchange(): lax.all_to_all(block.reshape(device_count, SLOTS, slide_width), ('seq', '...  19.2 us
    ppermute x12, starting transfers between devices, swap(): return lax.ppermute(value, 'seq', [(i, i ^ distance) for i in range(count)])  14.3 us
    all_to_all x2, waiting for transfers between devices, exchange(): lax.all_to_all(block.reshape(device_count, SLOTS, slide_width), ('seq', '...  12.6 us
    ppermute x12, waiting for transfers between devices, swap(): return lax.ppermute(value, 'seq', [(i, i ^ distance) for i in range(count)])  7.45 us
  transfers between devices with their start and end apart: 14, of which 4 were waited for; matrix products, arithmetic and copies ran while one was open for 0% of the time, Pallas kernels for 29%

profile of v1, /device:TPU:1, one launch (start us, length us, event | category | flops | bytes accessed | tf_op | source)
XLA Modules:
  0.0 115.9 jit_solution(12550333362688189425)
XLA Ops:
  0.6 11.8 %shard_map.104 = (bf16[8,128,768]{2,1,0:T(8,128)(2,1)}, bf16[128,768]{1,0:T(8,128)(2,1)}) custom-call(bf16[128,1536]{1,0:T(8,128)(2,1)} %feat_hbm.5, s32[128,128]{1,0:T(8,128)} %bitcast.9, bf16[1536,2048]{1,0:T(8,128)(2,1)} %gate_hbm.3, bf16[1536,2048]{1,0:T(8,128)(2,1)} %up_hbm.3, bf16[2048,1536]{1,0:T(8,128)(2,1)} %down_hbm.3, bf16[1536,768]{1,0:T(8,128)(2,1)} %proj_hbm.3, ...), custom_call_target="tpu_custom_call" | custom-call | tf_op jit(solution)/shard_map/pallas_call | solution.py:68
  12.4 11.5 %all-to-all-start = ((bf16[128,8,768]{2,1,0:T(8,128)(2,1)}), bf16[128,8,768]{2,1,0:T(8,128)(2,1)S(1)}, u32[]{:S(2)}, u32[]{:S(2)}) async-start(bf16[128,8,768]{2,1,0:T(8,128)(2,1)} %bitcast.14), calls=%async_computation | async-start | bytes 3145728 | tf_op jit(solution)/shard_map/all_to_all | solution.py:784
  23.9 0.0 copy-start.1
  23.9 11.7 %shard_map.106 = (bf16[2048,1536]{1,0:T(8,128)(2,1)}, bf16[2048,1536]{1,0:T(8,128)(2,1)}, bf16[128,2048]{1,0:T(8,128)(2,1)}, bf16[128,2048]{1,0:T(8,128)(2,1)}) custom-call(bf16[128,1536]{1,0:T(8,128)(2,1)} %feat_hbm.5, bf16[1536,2048]{1,0:T(8,128)(2,1)} %gate_hbm.3, bf16[1536,2048]{1,0:T(8,128)(2,1)} %up_hbm.3, ...), custom_call_target="tpu_custom_call" | custom-call | tf_op jit(solution)/shard_map/pallas_call | solution.py:68
  35.6 0.0 copy-start
  35.7 0.0 copy-start.3
  35.7 0.3 shard_map.109
  36.0 1.1 collective-permute-start.3
  37.1 0.8 collective-permute-start.4
  37.9 0.9 collective-permute-start.5
  38.9 0.9 shard_map.105
  39.8 9.5 %all-to-all-done = bf16[128,8,768]{2,1,0:T(8,128)(2,1)S(1)} async-done(((bf16[128,8,768]{2,1,0:T(8,128)(2,1)}), bf16[128,8,768]{2,1,0:T(8,128)(2,1)S(1)}, u32[]{:S(2)}, u32[]{:S(2)}) %all-to-all-start) | async-done | bytes 1572896 | tf_op jit(solution)/shard_map/all_to_all | solution.py:784
  49.3 1.9 %shard_map.107 = (bf16[4,512,192]{2,1,0:T(8,128)(2,1)S(1)}, bf16[4,192,512]{2,1,0:T(8,128)(2,1)S(1)}, bf16[128,192]{1,0:T(8,128)(2,1)S(1)}) custom-call(s32[2,16]{1,0:T(2,128)S(1)} %copy-done.3, bf16[1024,768]{1,0:T(8,128)(2,1)S(1)} %bitcast.8, s32[8,1024]{1,0:T(8,128)S(1)} %get-tuple-element.43.tab_ref, bf16[2048,1536]{1,0:T(8,128)(2,1)} %get-tuple-element.45._after_hbm.gate_hbm), custom_call_target="tpu_custom_call" | custom-call | tf_op jit(solution)/shard_map/pallas_call | solution.py:68
  51.2 0.1 collective-permute-start
  51.3 0.4 collective-permute-start.1
  51.8 3.7 %collective-permute-start.2 = (bf16[128,192]{1,0:T(8,128)(2,1)S(1)}, bf16[128,192]{1,0:T(8,128)(2,1)S(1)}, u32[]{:S(2)}, u32[]{:S(2)}) collective-permute-start(bf16[128,192]{1,0:T(8,128)(2,1)S(1)} %get-tuple-element.52.a0_ref), channel_id=1, source_target_pairs={{0,48},{4,52},{8,56},{12,60},{16,32},{20,36},{24,40},{28,44},{32,1... | collective-permute-start | bytes 147464 | tf_op jit(solution)/shard_map/ppermute | solution.py:760
  55.5 3.2 %shard_map.108 = (bf16[4,512,512]{2,1,0:T(8,128)(2,1)S(1)}, bf16[4,512,512]{2,1,0:T(8,128)(2,1)S(1)}, bf16[512,512]{1,0:T(8,128)(2,1)S(1)}, bf16[512,512]{1,0:T(...) custom-call(s32[2,16]{1,0:T(2,128)S(1)} %copy-done.3, ...), custom_call_target="tpu_custom_call" | custom-call | tf_op jit(solution)/shard_map/pallas_call | solution.py:68
  58.7 2.0 %shard_map.110 = (bf16[48,512]{1,0:T(8,128)(2,1)}, bf16[48,512]{1,0:T(8,128)(2,1)}, bf16[48,512]{1,0:T(8,128)(2,1)}, bf16[48,512]{1,0:T(8,128)(2,1)}, bf16[4,48,...) custom-call(s32[2,16]{1,0:T(2,128)S(1)} %copy-done.3, ...), custom_call_target="tpu_custom_call" | custom-call | tf_op jit(solution)/shard_map/pallas_call | solution.py:68
  60.7 1.5 %collective-permute-start.6 = (bf16[96,128]{1,0:T(8,128)(2,1)S(1)}, bf16[96,128]{1,0:T(8,128)(2,1)S(1)}, u32[]{:S(2)}, u32[]{:S(2)}) collective-permute-start(bf16[96,128]{1,0:T(8,128)(2,1)S(1)} %get-tuple-element.63), channel_id=1, source_target_pairs={{0,16},{4,20},{8,24},{12,28},{16,0},{20,4},{24,8},{28,12},{32,48},... | collective-permute-start | bytes 73736 | tf_op jit(solution)/shard_map/ppermute | solution.py:760
  62.2 1.1 collective-permute-start.7
  63.3 1.6 %collective-permute-start.8 = (bf16[96,128]{1,0:T(8,128)(2,1)S(1)}, bf16[96,128]{1,0:T(8,128)(2,1)S(1)}, u32[]{:S(2)}, u32[]{:S(2)}) collective-permute-start(bf16[96,128]{1,0:T(8,128)(2,1)S(1)} %get-tuple-element.65), channel_id=1, source_target_pairs={{0,48},{4,52},{8,56},{12,60},{16,32},{20,36},{24,40},{28,44},{32,1... | collective-permute-start | bytes 73736 | tf_op jit(solution)/shard_map/ppermute | solution.py:760
  65.0 3.8 %shard_map.111.dall_ref = f32[4,144,512]{2,1,0:T(8,128)S(1)} custom-call(s32[2,16]{1,0:T(2,128)S(1)} %copy-done.3, bf16[4,512,192]{2,1,0:T(8,128)(2,1)S(1)} %get-tuple-element.46.y_ref, bf16[4,192,512]{2,1,0:T(8,128)(2,1)S(1)} %get-tuple-element.47.yt_ref, bf16[4,512,512]{2,1,0:T(8,128)(2,1)S(1)} %get-tuple-element.48.e0_ref, ...), custom_call_target="tpu_custom_call" | custom-call | tf_op jit(solution)/shard_map/pallas_call | solution.py:68
  68.8 3.1 %shard_map.112._after_hbm = bf16[1024,768]{1,0:T(8,128)(2,1)} custom-call(s32[2,16]{1,0:T(2,128)S(1)} %copy-done.3, f32[4,144,512]{2,1,0:T(8,128)S(1)} %shard_map.111.dall_ref, f32[96,128]{1,0:T(8,128)S(1)} %get-tuple-element.61.own_ref, f32[48,128]{1,0:T(8,128)S(1)} %get-tuple-element.62.dq_ref, bf16[96,128]{1,0:T(8,128)(2,1)S(1)} %collective-permute-done.6.r1_ref, ...), custom_call_target="tpu_custom_call" | custom-call | tf_op jit(solution)/shard_map/pallas_call | solution.py:68
  71.8 7.7 %all-to-all-start.1 = ((bf16[128,8,768]{2,1,0:T(8,128)(2,1)}), bf16[128,8,768]{2,1,0:T(8,128)(2,1)S(1)}, u32[]{:S(2)}, u32[]{:S(2)}) async-start(bf16[128,8,768]{2,1,0:T(8,128)(2,1)} %bitcast.13), calls=%async_computation.1 | async-start | bytes 3145728 | tf_op jit(solution)/shard_map/all_to_all | solution.py:784
  79.6 0.0 copy-start.2
  79.6 11.8 %shard_map.113 = (bf16[768,2048]{1,0:T(8,128)(2,1)}, bf16[768,1536]{1,0:T(8,128)(2,1)}, bf16[2304,768]{1,0:T(8,128)(2,1)}, bf16[48,512]{1,0:T(8,128)(2,1)}, bf16...) custom-call(bf16[2048,1536]{1,0:T(8,128)(2,1)} %down_hbm.3, ...), custom_call_target="tpu_custom_call", output_to_operand_aliasing={{3}: (4, {}), {4}: (5, {}), {5}: (6, {})} | custom-call | tf_op jit(solution)/shard_map/pallas_call | solution.py:68
  91.5 1.8 %collective-permute-start.10 = (bf16[48,512]{1,0:T(8,128)(2,1)}, bf16[48,512]{1,0:T(8,128)(2,1)S(1)}, u32[]{:S(2)}, u32[]{:S(2)}) collective-permute-start(bf16[48,512]{1,0:T(8,128)(2,1)} %get-tuple-element.72), channel_id=1, source_target_pairs={{0,8},{4,12},{8,0},{12,4},{16,24},{20,28},{24,16},{28,20},{32,40},... | collective-permute-start | bytes 147464 | tf_op jit(solution)/shard_map/ppermute | solution.py:760
  93.3 1.2 %collective-permute-start.11 = (bf16[48,512]{1,0:T(8,128)(2,1)}, bf16[48,512]{1,0:T(8,128)(2,1)S(1)}, u32[]{:S(2)}, u32[]{:S(2)}) collective-permute-start(bf16[48,512]{1,0:T(8,128)(2,1)} %get-tuple-element.73), channel_id=1, source_target_pairs={{0,12},{4,8},{8,4},{12,0},{16,28},{20,24},{24,20},{28,16},{32,44},... | collective-permute-start | bytes 147464 | tf_op jit(solution)/shard_map/ppermute | solution.py:760
  94.5 3.4 %collective-permute-done.10.s2_any = bf16[48,512]{1,0:T(8,128)(2,1)S(1)} collective-permute-done((bf16[48,512]{1,0:T(8,128)(2,1)}, bf16[48,512]{1,0:T(8,128)(2,1)S(1)}, u32[]{:S(2)}, u32[]{:S(2)}) %collective-permute-start.10) | collective-permute-done | bytes 49184 | tf_op jit(solution)/shard_map/ppermute | solution.py:760
  97.8 4.1 %collective-permute-done.11.s3_any = bf16[48,512]{1,0:T(8,128)(2,1)S(1)} collective-permute-done((bf16[48,512]{1,0:T(8,128)(2,1)}, bf16[48,512]{1,0:T(8,128)(2,1)S(1)}, u32[]{:S(2)}, u32[]{:S(2)}) %collective-permute-start.11) | collective-permute-done | bytes 49184 | tf_op jit(solution)/shard_map/ppermute | solution.py:760
  101.9 3.1 %all-to-all-done.1 = bf16[128,8,768]{2,1,0:T(8,128)(2,1)S(1)} async-done(((bf16[128,8,768]{2,1,0:T(8,128)(2,1)}), bf16[128,8,768]{2,1,0:T(8,128)(2,1)S(1)}, u32[]{:S(2)}, u32[]{:S(2)}) %all-to-all-start.1) | async-done | bytes 1572896 | tf_op jit(solution)/shard_map/all_to_all | solution.py:784
  105.0 10.7 %shard_map.114 = (bf16[128,1536]{1,0:T(8,128)(2,1)}, bf16[192,512]{1,0:T(8,128)(2,1)}) custom-call(bf16[8,128,768]{2,1,0:T(8,128)(2,1)S(1)} %bitcast.7, bf16[48,512]{1,0:T(8,128)(2,1)S(1)} %copy-done.2, bf16[48,512]{1,0:T(8,128)(2,1)S(1)} %collective-permute-done.9.s1_any, bf16[48,512]{1,0:T(8,128)(2,1)S(1)} %collective-permute-done.10.s2_any, ...), custom_call_target="tpu_custom_call" | custom-call | tf_op jit(solution)/shard_map/pallas_call | solution.py:68
  (15 shorter events, 0.0 us)
Async XLA Ops:
  12.4 36.9 %all-to-all-start = ((bf16[128,8,768]{2,1,0:T(8,128)(2,1)}), bf16[128,8,768]{2,1,0:T(8,128)(2,1)S(1)}, u32[]{:S(2)}, u32[]{:S(2)}) async-start(bf16[128,8,768]{2,1,0:T(8,128)(2,1)} %bitcast.14), calls=%async_computation | async-start | bytes 3145728 | tf_op jit(solution)/shard_map/all_to_all | solution.py:784
  23.9 11.7 %copy-start.1 = (bf16[512,192]{0,1:T(8,128)(2,1)S(1)}, bf16[512,192]{0,1:T(8,128)(2,1)}, u32[]{:S(2)}) copy-start(bf16[512,192]{0,1:T(8,128)(2,1)} %param.17) | copy-start | bytes 589828
  35.6 3.2 %copy-start = (s32[16384]{0:T(1024)S(1)}, s32[16384]{0:T(1024)}, u32[]{:S(2)}) copy-start(s32[16384]{0:T(1024)} %param.15) | copy-start | bytes 196612
  35.7 13.7 %copy-start.3 = (s32[2,16]{1,0:T(2,128)S(1)}, s32[2,16]{1,0:T(2,128)}, u32[]{:S(2)}) copy-start(s32[2,16]{1,0:T(2,128)} %shift_ref.9) | copy-start | bytes 388
  36.0 15.8 %collective-permute-start.3 = (bf16[48,512]{1,0:T(8,128)(2,1)S(1)}, bf16[48,512]{1,0:T(8,128)(2,1)S(1)}, u32[]{:S(2)}, u32[]{:S(2)}) collective-permute-start(bf16[48,512]{1,0:T(8,128)(2,1)S(1)} %get-tuple-element.56), channel_id=1, source_target_pairs={{0,4},{4,0},{8,12},{12,8},{16,20},{20,16},{24,28},{28,24},{32,36},... | collective-permute-start | bytes 147464 | tf_op jit(solution)/shard_map/ppermute | solution.py:760
  37.1 21.6 %collective-permute-start.4 = (bf16[48,512]{1,0:T(8,128)(2,1)S(1)}, bf16[48,512]{1,0:T(8,128)(2,1)S(1)}, u32[]{:S(2)}, u32[]{:S(2)}) collective-permute-start(bf16[48,512]{1,0:T(8,128)(2,1)S(1)} %get-tuple-element.57), channel_id=1, source_target_pairs={{0,8},{4,12},{8,0},{12,4},{16,24},{20,28},{24,16},{28,20},{32,40},... | collective-permute-start | bytes 147464 | tf_op jit(solution)/shard_map/ppermute | solution.py:760
  37.9 20.8 %collective-permute-start.5 = (bf16[48,512]{1,0:T(8,128)(2,1)S(1)}, bf16[48,512]{1,0:T(8,128)(2,1)S(1)}, u32[]{:S(2)}, u32[]{:S(2)}) collective-permute-start(bf16[48,512]{1,0:T(8,128)(2,1)S(1)} %get-tuple-element.58), channel_id=1, source_target_pairs={{0,12},{4,8},{8,4},{12,0},{16,28},{20,24},{24,20},{28,16},{32,44},... | collective-permute-start | bytes 147464 | tf_op jit(solution)/shard_map/ppermute | solution.py:760
  51.2 7.5 %collective-permute-start = (bf16[128,192]{1,0:T(8,128)(2,1)S(1)}, bf16[128,192]{1,0:T(8,128)(2,1)S(1)}, u32[]{:S(2)}, u32[]{:S(2)}) collective-permute-start(bf16[128,192]{1,0:T(8,128)(2,1)S(1)} %get-tuple-element.52.a0_ref), channel_id=1, source_target_pairs={{0,16},{4,20},{8,24},{12,28},{16,0},{20,4},{24,8},{28,12},{32,48},... | collective-permute-start | bytes 147464 | tf_op jit(solution)/shard_map/ppermute | solution.py:760
  51.3 7.4 %collective-permute-start.1 = (bf16[128,192]{1,0:T(8,128)(2,1)S(1)}, bf16[128,192]{1,0:T(8,128)(2,1)S(1)}, u32[]{:S(2)}, u32[]{:S(2)}) collective-permute-start(bf16[128,192]{1,0:T(8,128)(2,1)S(1)} %get-tuple-element.52.a0_ref), channel_id=1, source_target_pairs={{0,32},{4,36},{8,40},{12,44},{16,48},{20,52},{24,56},{28,60},{32,0... | collective-permute-start | bytes 147464 | tf_op jit(solution)/shard_map/ppermute | solution.py:760
  51.8 7.0 %collective-permute-start.2 = (bf16[128,192]{1,0:T(8,128)(2,1)S(1)}, bf16[128,192]{1,0:T(8,128)(2,1)S(1)}, u32[]{:S(2)}, u32[]{:S(2)}) collective-permute-start(bf16[128,192]{1,0:T(8,128)(2,1)S(1)} %get-tuple-element.52.a0_ref), channel_id=1, source_target_pairs={{0,48},{4,52},{8,56},{12,60},{16,32},{20,36},{24,40},{28,44},{32,1... | collective-permute-start | bytes 147464 | tf_op jit(solution)/shard_map/ppermute | solution.py:760
  60.7 8.0 %collective-permute-start.6 = (bf16[96,128]{1,0:T(8,128)(2,1)S(1)}, bf16[96,128]{1,0:T(8,128)(2,1)S(1)}, u32[]{:S(2)}, u32[]{:S(2)}) collective-permute-start(bf16[96,128]{1,0:T(8,128)(2,1)S(1)} %get-tuple-element.63), channel_id=1, source_target_pairs={{0,16},{4,20},{8,24},{12,28},{16,0},{20,4},{24,8},{28,12},{32,48},... | collective-permute-start | bytes 73736 | tf_op jit(solution)/shard_map/ppermute | solution.py:760
  62.2 6.5 %collective-permute-start.7 = (bf16[96,128]{1,0:T(8,128)(2,1)S(1)}, bf16[96,128]{1,0:T(8,128)(2,1)S(1)}, u32[]{:S(2)}, u32[]{:S(2)}) collective-permute-start(bf16[96,128]{1,0:T(8,128)(2,1)S(1)} %get-tuple-element.64), channel_id=1, source_target_pairs={{0,32},{4,36},{8,40},{12,44},{16,48},{20,52},{24,56},{28,60},{32,0... | collective-permute-start | bytes 73736 | tf_op jit(solution)/shard_map/ppermute | solution.py:760
  63.3 5.4 %collective-permute-start.8 = (bf16[96,128]{1,0:T(8,128)(2,1)S(1)}, bf16[96,128]{1,0:T(8,128)(2,1)S(1)}, u32[]{:S(2)}, u32[]{:S(2)}) collective-permute-start(bf16[96,128]{1,0:T(8,128)(2,1)S(1)} %get-tuple-element.65), channel_id=1, source_target_pairs={{0,48},{4,52},{8,56},{12,60},{16,32},{20,36},{24,40},{28,44},{32,1... | collective-permute-start | bytes 73736 | tf_op jit(solution)/shard_map/ppermute | solution.py:760
  71.8 33.1 %all-to-all-start.1 = ((bf16[128,8,768]{2,1,0:T(8,128)(2,1)}), bf16[128,8,768]{2,1,0:T(8,128)(2,1)S(1)}, u32[]{:S(2)}, u32[]{:S(2)}) async-start(bf16[128,8,768]{2,1,0:T(8,128)(2,1)} %bitcast.13), calls=%async_computation.1 | async-start | bytes 3145728 | tf_op jit(solution)/shard_map/all_to_all | solution.py:784
  79.6 25.4 %copy-start.2 = (bf16[48,512]{1,0:T(8,128)(2,1)S(1)}, bf16[48,512]{1,0:T(8,128)(2,1)}, u32[]{:S(2)}) copy-start(bf16[48,512]{1,0:T(8,128)(2,1)} %get-tuple-element.67.s0_any) | copy-start | bytes 147460
  91.5 6.4 %collective-permute-start.10 = (bf16[48,512]{1,0:T(8,128)(2,1)}, bf16[48,512]{1,0:T(8,128)(2,1)S(1)}, u32[]{:S(2)}, u32[]{:S(2)}) collective-permute-start(bf16[48,512]{1,0:T(8,128)(2,1)} %get-tuple-element.72), channel_id=1, source_target_pairs={{0,8},{4,12},{8,0},{12,4},{16,24},{20,28},{24,16},{28,20},{32,40},... | collective-permute-start | bytes 147464 | tf_op jit(solution)/shard_map/ppermute | solution.py:760
  93.3 8.6 %collective-permute-start.11 = (bf16[48,512]{1,0:T(8,128)(2,1)}, bf16[48,512]{1,0:T(8,128)(2,1)S(1)}, u32[]{:S(2)}, u32[]{:S(2)}) collective-permute-start(bf16[48,512]{1,0:T(8,128)(2,1)} %get-tuple-element.73), channel_id=1, source_target_pairs={{0,12},{4,8},{8,4},{12,0},{16,28},{20,24},{24,20},{28,16},{32,44},... | collective-permute-start | bytes 147464 | tf_op jit(solution)/shard_map/ppermute | solution.py:760
  94.5 7.4 %collective-permute-start.9 = (bf16[48,512]{1,0:T(8,128)(2,1)}, bf16[48,512]{1,0:T(8,128)(2,1)S(1)}, u32[]{:S(2)}, u32[]{:S(2)}) collective-permute-start(bf16[48,512]{1,0:T(8,128)(2,1)} %get-tuple-element.71), channel_id=1, source_target_pairs={{0,4},{4,0},{8,12},{12,8},{16,20},{20,16},{24,28},{28,24},{32,36},... | collective-permute-start | bytes 147464 | tf_op jit(solution)/shard_map/ppermute | solution.py:760

commit v2 on v0

--- a/solution.py
+++ b/solution.py
@@ -567,10 +567,10 @@
     g1_ref,
     g2_ref,
     g3_ref,
-    so0_hbm,
-    so1_hbm,
-    so2_hbm,
-    so3_hbm,
+    so0_ref,
+    so1_ref,
+    so2_ref,
+    so3_ref,
     gs_ref,
     ds_ref,
     own_ref,
@@ -582,10 +582,7 @@
     m2_ref,
     usum_ref,
     lsum_ref,
-    so_ref,
-    so_sems,
 ):
-    outs = []
     _, base, part = offsets(shift_ref)
     base = pl.multiple_of(base, 128)
     y2 = jnp.concatenate([a0_ref[...], a1_ref[...], a2_ref[...], a3_ref[...]], axis=0)
@@ -614,9 +611,8 @@
         lsum_ref[:, pl.ds(base, 128)] += jnp.where(here, turned(l2w, shift), 0.0)[0:1]
         inv = 1.0 / lsum_ref[...]
         att = usum_ref[...] * inv
-        so_ref[d] = (yt_ref[d, 144:192, :].astype(F32) + att).astype(BF)
-        so = (so0_hbm, so1_hbm, so2_hbm, so3_hbm)[d]
-        outs += started([pltpu.make_async_copy(so_ref.at[d], so, so_sems.at[d])])
+        so_ref = (so0_ref, so1_ref, so2_ref, so3_ref)[d]
+        so_ref[...] = (yt_ref[d, 144:192, :].astype(F32) + att).astype(BF)
         grad_ref = (g0_ref, g1_ref, g2_ref, g3_ref)[d]
         gs = (grad_ref[...].astype(F32) * inv).astype(BF)
         gs_ref[d] = gs
@@ -635,7 +631,6 @@
     own_ref[...] = dkv[:, 0:128]
     for e, send_ref in enumerate((send1_ref, send2_ref, send3_ref)):
         send_ref[...] = dkv[:, 128 * e + 128 : 128 * e + 256].astype(BF)
-    finish(outs)
 
 
 def dscores(values, gs, ds, m_load, store):
@@ -646,8 +641,31 @@
 
 
 def backward_kernel(
-    shift_ref, y_ref, yt_ref, e0_ref, m0_ref, e1_ref, m1_ref, gs_ref, ds_ref, out_ref, tmp_ref
+    shift_ref,
+    y_ref,
+    yt_ref,
+    e0_ref,
+    m0_ref,
+    e1_ref,
+    m1_ref,
+    gs_ref,
+    ds_ref,
+    so0_ref,
+    so1_ref,
+    so2_ref,
+    so3_ref,
+    so0_hbm,
+    so1_hbm,
+    so2_hbm,
+    so3_hbm,
+    out_ref,
+    tmp_ref,
+    sems,
 ):
+    pairs = ((so0_ref, so0_hbm), (so1_ref, so1_hbm), (so2_ref, so2_hbm), (so3_ref, so3_hbm))
+    outs = started(
+        [pltpu.make_async_copy(here, there, sems.at[d]) for d, (here, there) in enumerate(pairs)]
+    )
     o1 = pl.multiple_of(offsets(shift_ref)[0], 128)
 
     def store(c, n, v):
@@ -676,6 +694,7 @@
     dall = jnp.concatenate([dq, dk, dv], axis=0)
     for d in range(4):
         out_ref[d, :, pl.ds(o1, 128)] += dall[:, 128 * d : 128 * d + 128]
+    finish(outs)
 
 
 def return_kernel(
@@ -706,8 +725,6 @@
     )
     extra = jnp.concatenate([dq_ref[...], dkv], axis=0)
     lane = iota((1, 128), 1) >> 5
-    rows = tab_ref.shape[0]
-    step = rows // 4
     outs, parts = [], []
     for d in range(4):
         grad_ref = (g0_ref, g1_ref, g2_ref, g3_ref)[d]
@@ -716,8 +733,8 @@
             lane == part, turned(extra, 32 * (part - d)), 0.0
         )
         parts.append(jnp.concatenate([sum_ref[...].astype(BF), grad_ref[...]], axis=0).T)
-    for c in range(4):
-        at = slice(step * c, step * c + step)
+    for c, (first, step) in enumerate(((0, 384), (384, 384), (768, 192), (960, 64))):
+        at = slice(first, first + step)
         for d in range(4):
             onehot = jnp.where(tab_ref[at, d : d + 1] == iota((step, BLK), 1), 1.0, 0.0)
             out_ref[at, 192 * d : 192 * d + 192] = mm(onehot.astype(BF), parts[d]).astype(BF)
@@ -842,19 +859,17 @@
             pltpu.VMEM((BLK, 128), BF),
             pltpu.VMEM((HD, BLK), F32),
             pltpu.VMEM((1, BLK), F32),
-            pltpu.VMEM((4, HD, BLK), BF),
-            dma((4,)),
         ],
         n_smem=1,
+    )(dilation_shift, yt, y2, *y2_in, u, l, *grads)
+    back = [swap(send, 4 * e, seq_count) for e, send in ((3, send3), (2, send2), (1, send1))]
+    *parts, dall = call(
+        backward_kernel,
+        [((HD, BLK), BF)] * 4 + [((4, 144, BLK), F32)],
+        [pltpu.VMEM((BLK, BLK), BF), dma((4,))],
+        n_smem=1,
         n_hbm_out=4,
-    )(dilation_shift, yt, y2, *y2_in, u, l, *grads)
-    back = [swap(send, 4 * e, seq_count) for e, send in ((1, send1), (2, send2), (3, send3))]
-    (dall,) = call(
-        backward_kernel,
-        [((4, 144, BLK), F32)],
-        [pltpu.VMEM((BLK, BLK), BF)],
-        n_smem=1,
-    )(dilation_shift, y, yt, e0, m0, e1, m1, gs, ds)
+    )(dilation_shift, y, yt, e0, m0, e1, m1, gs, ds, *parts)
     (returning,) = call(
         return_kernel,
         [((slots, slide_width), BF)],

time: 115 us -> 115 us (level)
  transfers between devices with their start and end apart: 14 -> 14, of which waited for: 3 -> 3; matrix products, arithmetic and copies ran while one was open for 0% -> 0% of each run, Pallas kernels for 27% -> 28%
where the time goes in v2:
time: 115 us
  Pallas kernels  58.8 us (51%)
  starting transfers between devices  32.6 us (28%)
  waiting for transfers between devices  22.4 us (19%)
    pallas_call x11, Pallas kernels, run(): pl.pallas_call(kernel, out_shape=shapes, in_specs=specs, out_specs=out_sp...  58.8 us
    all_to_all x2, starting transfers between devices, exchange(): lax.all_to_all(block.reshape(device_count, SLOTS, slide_width), ('seq', '...  18.4 us
    all_to_all x2, waiting for transfers between devices, exchange(): lax.all_to_all(block.reshape(device_count, SLOTS, slide_width), ('seq', '...  18.3 us
    ppermute x12, starting transfers between devices, swap(): return lax.ppermute(value, 'seq', [(i, i ^ distance) for i in range(count)])  14.2 us
    ppermute x12, waiting for transfers between devices, swap(): return lax.ppermute(value, 'seq', [(i, i ^ distance) for i in range(count)])  4.19 us
  transfers between devices with their start and end apart: 14, of which 3 were waited for; matrix products, arithmetic and copies ran while one was open for 0% of the time, Pallas kernels for 28%

profile of v2, /device:TPU:1, one launch (start us, length us, event | category | flops | bytes accessed | tf_op | source)
XLA Modules:
  0.0 114.9 jit_solution(6690222095637372864)
XLA Ops:
  0.6 11.8 %shard_map.104 = (bf16[8,128,768]{2,1,0:T(8,128)(2,1)}, bf16[128,768]{1,0:T(8,128)(2,1)}, bf16[128,2048]{1,0:T(8,128)(2,1)}, bf16[128,2048]{1,0:T(8,128)(2,1)}) custom-call(bf16[128,1536]{1,0:T(8,128)(2,1)} %feat_hbm.3, s32[128,128]{1,0:T(8,128)} %bitcast.9, bf16[1536,2048]{1,0:T(8,128)(2,1)} %gate_hbm.3, bf16[1536,2048]{1,0:T(8,128)(2,1)} %up_hbm.3, ...), custom_call_target="tpu_custom_call" | custom-call | tf_op jit(solution)/shard_map/pallas_call | solution.py:66
  12.4 0.0 copy-start.1
  12.4 0.0 copy-start
  12.4 11.5 %all-to-all-start = ((bf16[128,8,768]{2,1,0:T(8,128)(2,1)}), bf16[128,8,768]{2,1,0:T(8,128)(2,1)S(1)}, u32[]{:S(2)}, u32[]{:S(2)}) async-start(bf16[128,8,768]{2,1,0:T(8,128)(2,1)} %bitcast.14), calls=%async_computation | async-start | bytes 3145728 | tf_op jit(solution)/shard_map/all_to_all | solution.py:770
  23.9 0.3 shard_map.109
  24.3 1.1 collective-permute-start.3
  25.4 0.8 collective-permute-start.4
  26.2 0.9 collective-permute-start.5
  27.1 0.9 shard_map.105
  28.1 0.0 copy-start.3
  28.1 9.4 %shard_map.106 = (bf16[2048,1536]{1,0:T(8,128)(2,1)}, bf16[2048,1536]{1,0:T(8,128)(2,1)}) custom-call(bf16[1536,2048]{1,0:T(8,128)(2,1)} %gate_hbm.3, bf16[1536,2048]{1,0:T(8,128)(2,1)} %up_hbm.3, bf16[128,768]{1,0:T(8,128)(2,1)} %get-tuple-element.46._after_hbm.x_hbm), custom_call_target="tpu_custom_call" | custom-call | tf_op jit(solution)/shard_map/pallas_call | solution.py:66
  37.5 11.8 %all-to-all-done = bf16[128,8,768]{2,1,0:T(8,128)(2,1)S(1)} async-done(((bf16[128,8,768]{2,1,0:T(8,128)(2,1)}), bf16[128,8,768]{2,1,0:T(8,128)(2,1)S(1)}, u32[]{:S(2)}, u32[]{:S(2)}) %all-to-all-start) | async-done | bytes 1572896 | tf_op jit(solution)/shard_map/all_to_all | solution.py:770
  49.3 1.9 %shard_map.107 = (bf16[4,512,192]{2,1,0:T(8,128)(2,1)S(1)}, bf16[4,192,512]{2,1,0:T(8,128)(2,1)S(1)}, bf16[128,192]{1,0:T(8,128)(2,1)S(1)}) custom-call(s32[2,16]{1,0:T(2,128)S(1)} %copy-done.3, bf16[1024,768]{1,0:T(8,128)(2,1)S(1)} %bitcast.8, s32[8,1024]{1,0:T(8,128)S(1)} %get-tuple-element.45.tab_ref, bf16[2048,1536]{1,0:T(8,128)(2,1)} %get-tuple-element.47._after_hbm.gate_hbm), custom_call_target="tpu_custom_call" | custom-call | tf_op jit(solution)/shard_map/pallas_call | solution.py:66
  51.2 0.1 collective-permute-start.2
  51.3 1.0 collective-permute-start.1
  52.3 3.2 %collective-permute-start = (bf16[128,192]{1,0:T(8,128)(2,1)S(1)}, bf16[128,192]{1,0:T(8,128)(2,1)S(1)}, u32[]{:S(2)}, u32[]{:S(2)}) collective-permute-start(bf16[128,192]{1,0:T(8,128)(2,1)S(1)} %get-tuple-element.54.a0_ref), channel_id=1, source_target_pairs={{0,16},{4,20},{8,24},{12,28},{16,0},{20,4},{24,8},{28,12},{32,48},... | collective-permute-start | bytes 147464 | tf_op jit(solution)/shard_map/ppermute | solution.py:746
  55.5 3.2 %shard_map.108 = (bf16[4,512,512]{2,1,0:T(8,128)(2,1)S(1)}, bf16[4,512,512]{2,1,0:T(8,128)(2,1)S(1)}, bf16[512,512]{1,0:T(8,128)(2,1)S(1)}, bf16[512,512]{1,0:T(...) custom-call(s32[2,16]{1,0:T(2,128)S(1)} %copy-done.3, ...), custom_call_target="tpu_custom_call" | custom-call | tf_op jit(solution)/shard_map/pallas_call | solution.py:66
  58.7 1.7 %shard_map.110 = (bf16[48,512]{1,0:T(8,128)(2,1)S(1)}, bf16[48,512]{1,0:T(8,128)(2,1)S(1)}, bf16[48,512]{1,0:T(8,128)(2,1)S(1)}, bf16[48,512]{1,0:T(8,128)(2,1)S...) custom-call(s32[2,16]{1,0:T(2,128)S(1)} %copy-done.3, ...), custom_call_target="tpu_custom_call" | custom-call | tf_op jit(solution)/shard_map/pallas_call | solution.py:66
  60.4 1.5 %collective-permute-start.6 = (bf16[96,128]{1,0:T(8,128)(2,1)S(1)}, bf16[96,128]{1,0:T(8,128)(2,1)S(1)}, u32[]{:S(2)}, u32[]{:S(2)}) collective-permute-start(bf16[96,128]{1,0:T(8,128)(2,1)S(1)} %get-tuple-element.70), channel_id=1, source_target_pairs={{0,48},{4,52},{8,56},{12,60},{16,32},{20,36},{24,40},{28,44},{32,1... | collective-permute-start | bytes 73736 | tf_op jit(solution)/shard_map/ppermute | solution.py:746
  61.9 1.1 collective-permute-start.7
  63.0 1.6 %collective-permute-start.8 = (bf16[96,128]{1,0:T(8,128)(2,1)S(1)}, bf16[96,128]{1,0:T(8,128)(2,1)S(1)}, u32[]{:S(2)}, u32[]{:S(2)}) collective-permute-start(bf16[96,128]{1,0:T(8,128)(2,1)S(1)} %get-tuple-element.72), channel_id=1, source_target_pairs={{0,16},{4,20},{8,24},{12,28},{16,0},{20,4},{24,8},{28,12},{32,48},... | collective-permute-start | bytes 73736 | tf_op jit(solution)/shard_map/ppermute | solution.py:746
  64.7 4.0 %shard_map.111 = (bf16[48,512]{1,0:T(8,128)(2,1)}, bf16[48,512]{1,0:T(8,128)(2,1)}, bf16[48,512]{1,0:T(8,128)(2,1)}, bf16[48,512]{1,0:T(8,128)(2,1)}, f32[4,144,512]{2,1,0:T(8,128)S(1)}) custom-call(s32[2,16]{1,0:T(2,128)S(1)} %copy-done.3, bf16[4,512,192]{2,1,0:T(8,128)(2,1)S(1)} %get-tuple-element.48.y_ref, ...), custom_call_target="tpu_custom_call" | custom-call | tf_op jit(solution)/shard_map/pallas_call | solution.py:66
  68.7 3.0 %shard_map.112._after_hbm = bf16[1024,768]{1,0:T(8,128)(2,1)} custom-call(s32[2,16]{1,0:T(2,128)S(1)} %copy-done.3, f32[4,144,512]{2,1,0:T(8,128)S(1)} %get-tuple-element.67.dall_ref, f32[96,128]{1,0:T(8,128)S(1)} %get-tuple-element.68.own_ref, f32[48,128]{1,0:T(8,128)S(1)} %get-tuple-element.69.dq_ref, bf16[96,128]{1,0:T(8,128)(2,1)S(1)} %collective-permute-done.6.r1_ref, ...), custom_call_target="tpu_custom_call" | custom-call | tf_op jit(solution)/shard_map/pallas_call | solution.py:66
  71.7 0.0 copy-start.6
  71.8 6.9 %all-to-all-start.1 = ((bf16[128,8,768]{2,1,0:T(8,128)(2,1)}), bf16[128,8,768]{2,1,0:T(8,128)(2,1)S(1)}, u32[]{:S(2)}, u32[]{:S(2)}) async-start(bf16[128,8,768]{2,1,0:T(8,128)(2,1)} %bitcast.13), calls=%async_computation.1 | async-start | bytes 3145728 | tf_op jit(solution)/shard_map/all_to_all | solution.py:770
  78.6 1.1 collective-permute-start.9
  79.8 0.8 collective-permute-start.10
  80.6 0.9 collective-permute-start.11
  81.5 11.8 %shard_map.113 = (bf16[768,2048]{1,0:T(8,128)(2,1)}, bf16[768,1536]{1,0:T(8,128)(2,1)}, bf16[2304,768]{1,0:T(8,128)(2,1)}) custom-call(bf16[2048,1536]{1,0:T(8,128)(2,1)} %down_hbm.3, bf16[1536,768]{1,0:T(8,128)(2,1)} %proj_hbm.3, bf16[768,2304]{1,0:T(8,128)(2,1)} %qkvw_hbm.3, bf16[1024,768]{1,0:T(8,128)(2,1)} %shard_map.112._after_hbm), custom_call_target="tpu_custom_call" | custom-call | tf_op jit(solution)/shard_map/pallas_call | solution.py:66
  93.4 4.2 %collective-permute-done.11.s3_any = bf16[48,512]{1,0:T(8,128)(2,1)S(1)} collective-permute-done((bf16[48,512]{1,0:T(8,128)(2,1)S(1)}, bf16[48,512]{1,0:T(8,128)(2,1)S(1)}, u32[]{:S(2)}, u32[]{:S(2)}) %collective-permute-start.11) | collective-permute-done | bytes 49184 | tf_op jit(solution)/shard_map/ppermute | solution.py:746
  97.5 6.5 %all-to-all-done.1 = bf16[128,8,768]{2,1,0:T(8,128)(2,1)S(1)} async-done(((bf16[128,8,768]{2,1,0:T(8,128)(2,1)}), bf16[128,8,768]{2,1,0:T(8,128)(2,1)S(1)}, u32[]{:S(2)}, u32[]{:S(2)}) %all-to-all-start.1) | async-done | bytes 1572896 | tf_op jit(solution)/shard_map/all_to_all | solution.py:770
  104.0 10.7 %shard_map.114 = (bf16[128,1536]{1,0:T(8,128)(2,1)}, bf16[192,512]{1,0:T(8,128)(2,1)}) custom-call(bf16[8,128,768]{2,1,0:T(8,128)(2,1)S(1)} %bitcast.7, bf16[48,512]{1,0:T(8,128)(2,1)S(1)} %copy-done.2, bf16[48,512]{1,0:T(8,128)(2,1)S(1)} %collective-permute-done.9.s1_any, bf16[48,512]{1,0:T(8,128)(2,1)S(1)} %collective-permute-done.10.s2_any, ...), custom_call_target="tpu_custom_call" | custom-call | tf_op jit(solution)/shard_map/pallas_call | solution.py:66
  (21 shorter events, 0.0 us)
Async XLA Ops:
  12.4 11.5 %copy-start.1 = (bf16[512,192]{0,1:T(8,128)(2,1)S(1)}, bf16[512,192]{0,1:T(8,128)(2,1)}, u32[]{:S(2)}) copy-start(bf16[512,192]{0,1:T(8,128)(2,1)} %param.17) | copy-start | bytes 589828
  12.4 14.7 %copy-start = (s32[16384]{0:T(1024)S(1)}, s32[16384]{0:T(1024)}, u32[]{:S(2)}) copy-start(s32[16384]{0:T(1024)} %param.15) | copy-start | bytes 196612
  12.4 36.9 %all-to-all-start = ((bf16[128,8,768]{2,1,0:T(8,128)(2,1)}), bf16[128,8,768]{2,1,0:T(8,128)(2,1)S(1)}, u32[]{:S(2)}, u32[]{:S(2)}) async-start(bf16[128,8,768]{2,1,0:T(8,128)(2,1)} %bitcast.14), calls=%async_computation | async-start | bytes 3145728 | tf_op jit(solution)/shard_map/all_to_all | solution.py:770
  24.3 28.0 %collective-permute-start.3 = (bf16[48,512]{1,0:T(8,128)(2,1)S(1)}, bf16[48,512]{1,0:T(8,128)(2,1)S(1)}, u32[]{:S(2)}, u32[]{:S(2)}) collective-permute-start(bf16[48,512]{1,0:T(8,128)(2,1)S(1)} %get-tuple-element.58), channel_id=1, source_target_pairs={{0,4},{4,0},{8,12},{12,8},{16,20},{20,16},{24,28},{28,24},{32,36},... | collective-permute-start | bytes 147464 | tf_op jit(solution)/shard_map/ppermute | solution.py:746
  25.4 33.3 %collective-permute-start.4 = (bf16[48,512]{1,0:T(8,128)(2,1)S(1)}, bf16[48,512]{1,0:T(8,128)(2,1)S(1)}, u32[]{:S(2)}, u32[]{:S(2)}) collective-permute-start(bf16[48,512]{1,0:T(8,128)(2,1)S(1)} %get-tuple-element.59), channel_id=1, source_target_pairs={{0,8},{4,12},{8,0},{12,4},{16,24},{20,28},{24,16},{28,20},{32,40},... | collective-permute-start | bytes 147464 | tf_op jit(solution)/shard_map/ppermute | solution.py:746
  26.2 32.5 %collective-permute-start.5 = (bf16[48,512]{1,0:T(8,128)(2,1)S(1)}, bf16[48,512]{1,0:T(8,128)(2,1)S(1)}, u32[]{:S(2)}, u32[]{:S(2)}) collective-permute-start(bf16[48,512]{1,0:T(8,128)(2,1)S(1)} %get-tuple-element.60), channel_id=1, source_target_pairs={{0,12},{4,8},{8,4},{12,0},{16,28},{20,24},{24,20},{28,16},{32,44},... | collective-permute-start | bytes 147464 | tf_op jit(solution)/shard_map/ppermute | solution.py:746
  28.1 21.2 %copy-start.3 = (s32[2,16]{1,0:T(2,128)S(1)}, s32[2,16]{1,0:T(2,128)}, u32[]{:S(2)}) copy-start(s32[2,16]{1,0:T(2,128)} %shift_ref.9) | copy-start | bytes 388
  51.2 7.5 %collective-permute-start.2 = (bf16[128,192]{1,0:T(8,128)(2,1)S(1)}, bf16[128,192]{1,0:T(8,128)(2,1)S(1)}, u32[]{:S(2)}, u32[]{:S(2)}) collective-permute-start(bf16[128,192]{1,0:T(8,128)(2,1)S(1)} %get-tuple-element.54.a0_ref), channel_id=1, source_target_pairs={{0,48},{4,52},{8,56},{12,60},{16,32},{20,36},{24,40},{28,44},{32,1... | collective-permute-start | bytes 147464 | tf_op jit(solution)/shard_map/ppermute | solution.py:746
  51.3 7.4 %collective-permute-start.1 = (bf16[128,192]{1,0:T(8,128)(2,1)S(1)}, bf16[128,192]{1,0:T(8,128)(2,1)S(1)}, u32[]{:S(2)}, u32[]{:S(2)}) collective-permute-start(bf16[128,192]{1,0:T(8,128)(2,1)S(1)} %get-tuple-element.54.a0_ref), channel_id=1, source_target_pairs={{0,32},{4,36},{8,40},{12,44},{16,48},{20,52},{24,56},{28,60},{32,0... | collective-permute-start | bytes 147464 | tf_op jit(solution)/shard_map/ppermute | solution.py:746
  52.3 6.4 %collective-permute-start = (bf16[128,192]{1,0:T(8,128)(2,1)S(1)}, bf16[128,192]{1,0:T(8,128)(2,1)S(1)}, u32[]{:S(2)}, u32[]{:S(2)}) collective-permute-start(bf16[128,192]{1,0:T(8,128)(2,1)S(1)} %get-tuple-element.54.a0_ref), channel_id=1, source_target_pairs={{0,16},{4,20},{8,24},{12,28},{16,0},{20,4},{24,8},{28,12},{32,48},... | collective-permute-start | bytes 147464 | tf_op jit(solution)/shard_map/ppermute | solution.py:746
  60.4 8.2 %collective-permute-start.6 = (bf16[96,128]{1,0:T(8,128)(2,1)S(1)}, bf16[96,128]{1,0:T(8,128)(2,1)S(1)}, u32[]{:S(2)}, u32[]{:S(2)}) collective-permute-start(bf16[96,128]{1,0:T(8,128)(2,1)S(1)} %get-tuple-element.70), channel_id=1, source_target_pairs={{0,48},{4,52},{8,56},{12,60},{16,32},{20,36},{24,40},{28,44},{32,1... | collective-permute-start | bytes 73736 | tf_op jit(solution)/shard_map/ppermute | solution.py:746
  61.9 6.8 %collective-permute-start.7 = (bf16[96,128]{1,0:T(8,128)(2,1)S(1)}, bf16[96,128]{1,0:T(8,128)(2,1)S(1)}, u32[]{:S(2)}, u32[]{:S(2)}) collective-permute-start(bf16[96,128]{1,0:T(8,128)(2,1)S(1)} %get-tuple-element.71), channel_id=1, source_target_pairs={{0,32},{4,36},{8,40},{12,44},{16,48},{20,52},{24,56},{28,60},{32,0... | collective-permute-start | bytes 73736 | tf_op jit(solution)/shard_map/ppermute | solution.py:746
  63.0 5.7 %collective-permute-start.8 = (bf16[96,128]{1,0:T(8,128)(2,1)S(1)}, bf16[96,128]{1,0:T(8,128)(2,1)S(1)}, u32[]{:S(2)}, u32[]{:S(2)}) collective-permute-start(bf16[96,128]{1,0:T(8,128)(2,1)S(1)} %get-tuple-element.72), channel_id=1, source_target_pairs={{0,16},{4,20},{8,24},{12,28},{16,0},{20,4},{24,8},{28,12},{32,48},... | collective-permute-start | bytes 73736 | tf_op jit(solution)/shard_map/ppermute | solution.py:746
  71.7 6.9 %copy-start.6 = (bf16[48,512]{1,0:T(8,128)(2,1)S(1)}, bf16[48,512]{1,0:T(8,128)(2,1)}, u32[]{:S(2)}) copy-start(bf16[48,512]{1,0:T(8,128)(2,1)} %get-tuple-element.75) | copy-start | bytes 147460
  71.7 8.0 %copy-start.5 = (bf16[48,512]{1,0:T(8,128)(2,1)S(1)}, bf16[48,512]{1,0:T(8,128)(2,1)}, u32[]{:S(2)}) copy-start(bf16[48,512]{1,0:T(8,128)(2,1)} %get-tuple-element.76) | copy-start | bytes 147460
  71.8 8.8 %copy-start.4 = (bf16[48,512]{1,0:T(8,128)(2,1)S(1)}, bf16[48,512]{1,0:T(8,128)(2,1)}, u32[]{:S(2)}) copy-start(bf16[48,512]{1,0:T(8,128)(2,1)} %get-tuple-element.77) | copy-start | bytes 147460
  71.8 32.2 %all-to-all-start.1 = ((bf16[128,8,768]{2,1,0:T(8,128)(2,1)}), bf16[128,8,768]{2,1,0:T(8,128)(2,1)S(1)}, u32[]{:S(2)}, u32[]{:S(2)}) async-start(bf16[128,8,768]{2,1,0:T(8,128)(2,1)} %bitcast.13), calls=%async_computation.1 | async-start | bytes 3145728 | tf_op jit(solution)/shard_map/all_to_all | solution.py:770
  78.6 14.7 %collective-permute-start.9 = (bf16[48,512]{1,0:T(8,128)(2,1)S(1)}, bf16[48,512]{1,0:T(8,128)(2,1)S(1)}, u32[]{:S(2)}, u32[]{:S(2)}) collective-permute-start(bf16[48,512]{1,0:T(8,128)(2,1)S(1)} %copy-done.6), channel_id=1, source_target_pairs={{0,4},{4,0},{8,12},{12,8},{16,20},{20,16},{24,28},{28,24},{32,36},... | collective-permute-start | bytes 147464 | tf_op jit(solution)/shard_map/ppermute | solution.py:746
  79.8 13.6 %collective-permute-start.10 = (bf16[48,512]{1,0:T(8,128)(2,1)S(1)}, bf16[48,512]{1,0:T(8,128)(2,1)S(1)}, u32[]{:S(2)}, u32[]{:S(2)}) collective-permute-start(bf16[48,512]{1,0:T(8,128)(2,1)S(1)} %copy-done.5), channel_id=1, source_target_pairs={{0,8},{4,12},{8,0},{12,4},{16,24},{20,28},{24,16},{28,20},{32,40},... | collective-permute-start | bytes 147464 | tf_op jit(solution)/shard_map/ppermute | solution.py:746
  80.6 23.4 %copy-start.2 = (bf16[48,512]{1,0:T(8,128)(2,1)S(1)}, bf16[48,512]{1,0:T(8,128)(2,1)}, u32[]{:S(2)}) copy-start(bf16[48,512]{1,0:T(8,128)(2,1)} %get-tuple-element.74.s0_any) | copy-start | bytes 147460
  80.6 16.9 %collective-permute-start.11 = (bf16[48,512]{1,0:T(8,128)(2,1)S(1)}, bf16[48,512]{1,0:T(8,128)(2,1)S(1)}, u32[]{:S(2)}, u32[]{:S(2)}) collective-permute-start(bf16[48,512]{1,0:T(8,128)(2,1)S(1)} %copy-done.4), channel_id=1, source_target_pairs={{0,12},{4,8},{8,4},{12,0},{16,28},{20,24},{24,20},{28,16},{32,44},... | collective-permute-start | bytes 147464 | tf_op jit(solution)/shard_map/ppermute | solution.py:746

commit v3 on v2

--- a/solution.py
+++ b/solution.py
@@ -511,7 +511,7 @@
     step = 128
     for c in range(0, count, step):
         t = jnp.tanh(mm(keys[c : c + step], queries_t) * (SCALE / SOFT_CAP))
-        e = jnp.exp2((SOFT_CAP * LOG2_E) * t)
+        e = jnp.exp2((SOFT_CAP * LOG2_E) * t - 17.0)
         total = total + jnp.sum(e.reshape(step // 8, 8, width), axis=0)
         e_store(c, step, e.astype(BF))
         m_store(c, step, (e - e * (t * t)).astype(BF))

time: 115 us -> 115 us (level)
  no operation moved by 1% of the time
where the time goes in v3:
time: 115 us
  Pallas kernels  59 us (51%)
  starting transfers between devices  32.4 us (28%)
  waiting for transfers between devices  22.4 us (19%)
    pallas_call x11, Pallas kernels, run(): pl.pallas_call(kernel, out_shape=shapes, in_specs=specs, out_specs=out_sp...  59 us
    all_to_all x2, waiting for transfers between devices, exchange(): lax.all_to_all(block.reshape(device_count, SLOTS, slide_width), ('seq', '...  18.3 us
    all_to_all x2, starting transfers between devices, exchange(): lax.all_to_all(block.reshape(device_count, SLOTS, slide_width), ('seq', '...  18.2 us
    ppermute x12, starting transfers between devices, swap(): return lax.ppermute(value, 'seq', [(i, i ^ distance) for i in range(count)])  14.2 us
    ppermute x12, waiting for transfers between devices, swap(): return lax.ppermute(value, 'seq', [(i, i ^ distance) for i in range(count)])  4.19 us
  transfers between devices with their start and end apart: 14, of which 3 were waited for; matrix products, arithmetic and copies ran while one was open for 0% of the time, Pallas kernels for 28%

profile of v3, /device:TPU:1, one launch (start us, length us, event | category | flops | bytes accessed | tf_op | source)
XLA Modules:
  0.0 114.9 jit_solution(14926925974408776871)
XLA Ops:
  0.6 11.8 %shard_map.104 = (bf16[8,128,768]{2,1,0:T(8,128)(2,1)}, bf16[128,768]{1,0:T(8,128)(2,1)}, bf16[128,2048]{1,0:T(8,128)(2,1)}, bf16[128,2048]{1,0:T(8,128)(2,1)}) custom-call(bf16[128,1536]{1,0:T(8,128)(2,1)} %feat_hbm.3, s32[128,128]{1,0:T(8,128)} %bitcast.9, bf16[1536,2048]{1,0:T(8,128)(2,1)} %gate_hbm.3, bf16[1536,2048]{1,0:T(8,128)(2,1)} %up_hbm.3, ...), custom_call_target="tpu_custom_call" | custom-call | tf_op jit(solution)/shard_map/pallas_call | solution.py:66
  12.4 0.0 copy-start.1
  12.4 0.0 copy-start
  12.4 11.5 %all-to-all-start = ((bf16[128,8,768]{2,1,0:T(8,128)(2,1)}), bf16[128,8,768]{2,1,0:T(8,128)(2,1)S(1)}, u32[]{:S(2)}, u32[]{:S(2)}) async-start(bf16[128,8,768]{2,1,0:T(8,128)(2,1)} %bitcast.14), calls=%async_computation | async-start | bytes 3145728 | tf_op jit(solution)/shard_map/all_to_all | solution.py:770
  23.9 0.3 shard_map.109
  24.3 1.1 collective-permute-start.3
  25.4 0.8 collective-permute-start.4
  26.2 0.9 collective-permute-start.5
  27.1 0.9 shard_map.105
  28.1 0.0 copy-start.3
  28.1 9.4 %shard_map.106 = (bf16[2048,1536]{1,0:T(8,128)(2,1)}, bf16[2048,1536]{1,0:T(8,128)(2,1)}) custom-call(bf16[1536,2048]{1,0:T(8,128)(2,1)} %gate_hbm.3, bf16[1536,2048]{1,0:T(8,128)(2,1)} %up_hbm.3, bf16[128,768]{1,0:T(8,128)(2,1)} %get-tuple-element.46._after_hbm.x_hbm), custom_call_target="tpu_custom_call" | custom-call | tf_op jit(solution)/shard_map/pallas_call | solution.py:66
  37.5 11.8 %all-to-all-done = bf16[128,8,768]{2,1,0:T(8,128)(2,1)S(1)} async-done(((bf16[128,8,768]{2,1,0:T(8,128)(2,1)}), bf16[128,8,768]{2,1,0:T(8,128)(2,1)S(1)}, u32[]{:S(2)}, u32[]{:S(2)}) %all-to-all-start) | async-done | bytes 1572896 | tf_op jit(solution)/shard_map/all_to_all | solution.py:770
  49.3 1.9 %shard_map.107 = (bf16[4,512,192]{2,1,0:T(8,128)(2,1)S(1)}, bf16[4,192,512]{2,1,0:T(8,128)(2,1)S(1)}, bf16[128,192]{1,0:T(8,128)(2,1)S(1)}) custom-call(s32[2,16]{1,0:T(2,128)S(1)} %copy-done.3, bf16[1024,768]{1,0:T(8,128)(2,1)S(1)} %bitcast.8, s32[8,1024]{1,0:T(8,128)S(1)} %get-tuple-element.45.tab_ref, bf16[2048,1536]{1,0:T(8,128)(2,1)} %get-tuple-element.47._after_hbm.gate_hbm), custom_call_target="tpu_custom_call" | custom-call | tf_op jit(solution)/shard_map/pallas_call | solution.py:66
  51.2 0.1 collective-permute-start.2
  51.3 1.0 collective-permute-start.1
  52.3 3.2 %collective-permute-start = (bf16[128,192]{1,0:T(8,128)(2,1)S(1)}, bf16[128,192]{1,0:T(8,128)(2,1)S(1)}, u32[]{:S(2)}, u32[]{:S(2)}) collective-permute-start(bf16[128,192]{1,0:T(8,128)(2,1)S(1)} %get-tuple-element.54.a0_ref), channel_id=1, source_target_pairs={{0,16},{4,20},{8,24},{12,28},{16,0},{20,4},{24,8},{28,12},{32,48},... | collective-permute-start | bytes 147464 | tf_op jit(solution)/shard_map/ppermute | solution.py:746
  55.5 3.4 %shard_map.108 = (bf16[4,512,512]{2,1,0:T(8,128)(2,1)S(1)}, bf16[4,512,512]{2,1,0:T(8,128)(2,1)S(1)}, bf16[512,512]{1,0:T(8,128)(2,1)S(1)}, bf16[512,512]{1,0:T(...) custom-call(s32[2,16]{1,0:T(2,128)S(1)} %copy-done.3, ...), custom_call_target="tpu_custom_call" | custom-call | tf_op jit(solution)/shard_map/pallas_call | solution.py:66
  58.9 1.7 %shard_map.110 = (bf16[48,512]{1,0:T(8,128)(2,1)S(1)}, bf16[48,512]{1,0:T(8,128)(2,1)S(1)}, bf16[48,512]{1,0:T(8,128)(2,1)S(1)}, bf16[48,512]{1,0:T(8,128)(2,1)S...) custom-call(s32[2,16]{1,0:T(2,128)S(1)} %copy-done.3, ...), custom_call_target="tpu_custom_call" | custom-call | tf_op jit(solution)/shard_map/pallas_call | solution.py:66
  60.6 1.3 %collective-permute-start.6 = (bf16[96,128]{1,0:T(8,128)(2,1)S(1)}, bf16[96,128]{1,0:T(8,128)(2,1)S(1)}, u32[]{:S(2)}, u32[]{:S(2)}) collective-permute-start(bf16[96,128]{1,0:T(8,128)(2,1)S(1)} %get-tuple-element.70), channel_id=1, source_target_pairs={{0,48},{4,52},{8,56},{12,60},{16,32},{20,36},{24,40},{28,44},{32,1... | collective-permute-start | bytes 73736 | tf_op jit(solution)/shard_map/ppermute | solution.py:746
  61.9 1.1 collective-permute-start.7
  63.0 1.8 %collective-permute-start.8 = (bf16[96,128]{1,0:T(8,128)(2,1)S(1)}, bf16[96,128]{1,0:T(8,128)(2,1)S(1)}, u32[]{:S(2)}, u32[]{:S(2)}) collective-permute-start(bf16[96,128]{1,0:T(8,128)(2,1)S(1)} %get-tuple-element.72), channel_id=1, source_target_pairs={{0,16},{4,20},{8,24},{12,28},{16,0},{20,4},{24,8},{28,12},{32,48},... | collective-permute-start | bytes 73736 | tf_op jit(solution)/shard_map/ppermute | solution.py:746
  64.9 4.0 %shard_map.111 = (bf16[48,512]{1,0:T(8,128)(2,1)}, bf16[48,512]{1,0:T(8,128)(2,1)}, bf16[48,512]{1,0:T(8,128)(2,1)}, bf16[48,512]{1,0:T(8,128)(2,1)}, f32[4,144,512]{2,1,0:T(8,128)S(1)}) custom-call(s32[2,16]{1,0:T(2,128)S(1)} %copy-done.3, bf16[4,512,192]{2,1,0:T(8,128)(2,1)S(1)} %get-tuple-element.48.y_ref, ...), custom_call_target="tpu_custom_call" | custom-call | tf_op jit(solution)/shard_map/pallas_call | solution.py:66
  68.9 3.0 %shard_map.112._after_hbm = bf16[1024,768]{1,0:T(8,128)(2,1)} custom-call(s32[2,16]{1,0:T(2,128)S(1)} %copy-done.3, f32[4,144,512]{2,1,0:T(8,128)S(1)} %get-tuple-element.67.dall_ref, f32[96,128]{1,0:T(8,128)S(1)} %get-tuple-element.68.own_ref, f32[48,128]{1,0:T(8,128)S(1)} %get-tuple-element.69.dq_ref, bf16[96,128]{1,0:T(8,128)(2,1)S(1)} %collective-permute-done.6.r1_ref, ...), custom_call_target="tpu_custom_call" | custom-call | tf_op jit(solution)/shard_map/pallas_call | solution.py:66
  71.9 0.0 copy-start.6
  72.0 6.7 %all-to-all-start.1 = ((bf16[128,8,768]{2,1,0:T(8,128)(2,1)}), bf16[128,8,768]{2,1,0:T(8,128)(2,1)S(1)}, u32[]{:S(2)}, u32[]{:S(2)}) async-start(bf16[128,8,768]{2,1,0:T(8,128)(2,1)} %bitcast.13), calls=%async_computation.1 | async-start | bytes 3145728 | tf_op jit(solution)/shard_map/all_to_all | solution.py:770
  78.7 1.1 collective-permute-start.9
  79.8 0.8 collective-permute-start.10
  80.6 0.9 collective-permute-start.11
  81.5 11.8 %shard_map.113 = (bf16[768,2048]{1,0:T(8,128)(2,1)}, bf16[768,1536]{1,0:T(8,128)(2,1)}, bf16[2304,768]{1,0:T(8,128)(2,1)}) custom-call(bf16[2048,1536]{1,0:T(8,128)(2,1)} %down_hbm.3, bf16[1536,768]{1,0:T(8,128)(2,1)} %proj_hbm.3, bf16[768,2304]{1,0:T(8,128)(2,1)} %qkvw_hbm.3, bf16[1024,768]{1,0:T(8,128)(2,1)} %shard_map.112._after_hbm), custom_call_target="tpu_custom_call" | custom-call | tf_op jit(solution)/shard_map/pallas_call | solution.py:66
  93.4 4.2 %collective-permute-done.11.s3_any = bf16[48,512]{1,0:T(8,128)(2,1)S(1)} collective-permute-done((bf16[48,512]{1,0:T(8,128)(2,1)S(1)}, bf16[48,512]{1,0:T(8,128)(2,1)S(1)}, u32[]{:S(2)}, u32[]{:S(2)}) %collective-permute-start.11) | collective-permute-done | bytes 49184 | tf_op jit(solution)/shard_map/ppermute | solution.py:746
  97.6 6.5 %all-to-all-done.1 = bf16[128,8,768]{2,1,0:T(8,128)(2,1)S(1)} async-done(((bf16[128,8,768]{2,1,0:T(8,128)(2,1)}), bf16[128,8,768]{2,1,0:T(8,128)(2,1)S(1)}, u32[]{:S(2)}, u32[]{:S(2)}) %all-to-all-start.1) | async-done | bytes 1572896 | tf_op jit(solution)/shard_map/all_to_all | solution.py:770
  104.0 10.7 %shard_map.114 = (bf16[128,1536]{1,0:T(8,128)(2,1)}, bf16[192,512]{1,0:T(8,128)(2,1)}) custom-call(bf16[8,128,768]{2,1,0:T(8,128)(2,1)S(1)} %bitcast.7, bf16[48,512]{1,0:T(8,128)(2,1)S(1)} %copy-done.2, bf16[48,512]{1,0:T(8,128)(2,1)S(1)} %collective-permute-done.9.s1_any, bf16[48,512]{1,0:T(8,128)(2,1)S(1)} %collective-permute-done.10.s2_any, ...), custom_call_target="tpu_custom_call" | custom-call | tf_op jit(solution)/shard_map/pallas_call | solution.py:66
  (21 shorter events, 0.0 us)
Async XLA Ops:
  12.4 11.5 %copy-start.1 = (bf16[512,192]{0,1:T(8,128)(2,1)S(1)}, bf16[512,192]{0,1:T(8,128)(2,1)}, u32[]{:S(2)}) copy-start(bf16[512,192]{0,1:T(8,128)(2,1)} %param.17) | copy-start | bytes 589828
  12.4 14.7 %copy-start = (s32[16384]{0:T(1024)S(1)}, s32[16384]{0:T(1024)}, u32[]{:S(2)}) copy-start(s32[16384]{0:T(1024)} %param.15) | copy-start | bytes 196612
  12.4 36.9 %all-to-all-start = ((bf16[128,8,768]{2,1,0:T(8,128)(2,1)}), bf16[128,8,768]{2,1,0:T(8,128)(2,1)S(1)}, u32[]{:S(2)}, u32[]{:S(2)}) async-start(bf16[128,8,768]{2,1,0:T(8,128)(2,1)} %bitcast.14), calls=%async_computation | async-start | bytes 3145728 | tf_op jit(solution)/shard_map/all_to_all | solution.py:770
  24.3 28.0 %collective-permute-start.3 = (bf16[48,512]{1,0:T(8,128)(2,1)S(1)}, bf16[48,512]{1,0:T(8,128)(2,1)S(1)}, u32[]{:S(2)}, u32[]{:S(2)}) collective-permute-start(bf16[48,512]{1,0:T(8,128)(2,1)S(1)} %get-tuple-element.58), channel_id=1, source_target_pairs={{0,4},{4,0},{8,12},{12,8},{16,20},{20,16},{24,28},{28,24},{32,36},... | collective-permute-start | bytes 147464 | tf_op jit(solution)/shard_map/ppermute | solution.py:746
  25.4 33.5 %collective-permute-start.4 = (bf16[48,512]{1,0:T(8,128)(2,1)S(1)}, bf16[48,512]{1,0:T(8,128)(2,1)S(1)}, u32[]{:S(2)}, u32[]{:S(2)}) collective-permute-start(bf16[48,512]{1,0:T(8,128)(2,1)S(1)} %get-tuple-element.59), channel_id=1, source_target_pairs={{0,8},{4,12},{8,0},{12,4},{16,24},{20,28},{24,16},{28,20},{32,40},... | collective-permute-start | bytes 147464 | tf_op jit(solution)/shard_map/ppermute | solution.py:746
  26.2 32.7 %collective-permute-start.5 = (bf16[48,512]{1,0:T(8,128)(2,1)S(1)}, bf16[48,512]{1,0:T(8,128)(2,1)S(1)}, u32[]{:S(2)}, u32[]{:S(2)}) collective-permute-start(bf16[48,512]{1,0:T(8,128)(2,1)S(1)} %get-tuple-element.60), channel_id=1, source_target_pairs={{0,12},{4,8},{8,4},{12,0},{16,28},{20,24},{24,20},{28,16},{32,44},... | collective-permute-start | bytes 147464 | tf_op jit(solution)/shard_map/ppermute | solution.py:746
  28.1 21.2 %copy-start.3 = (s32[2,16]{1,0:T(2,128)S(1)}, s32[2,16]{1,0:T(2,128)}, u32[]{:S(2)}) copy-start(s32[2,16]{1,0:T(2,128)} %shift_ref.9) | copy-start | bytes 388
  51.2 7.7 %collective-permute-start.2 = (bf16[128,192]{1,0:T(8,128)(2,1)S(1)}, bf16[128,192]{1,0:T(8,128)(2,1)S(1)}, u32[]{:S(2)}, u32[]{:S(2)}) collective-permute-start(bf16[128,192]{1,0:T(8,128)(2,1)S(1)} %get-tuple-element.54.a0_ref), channel_id=1, source_target_pairs={{0,48},{4,52},{8,56},{12,60},{16,32},{20,36},{24,40},{28,44},{32,1... | collective-permute-start | bytes 147464 | tf_op jit(solution)/shard_map/ppermute | solution.py:746
  51.3 7.6 %collective-permute-start.1 = (bf16[128,192]{1,0:T(8,128)(2,1)S(1)}, bf16[128,192]{1,0:T(8,128)(2,1)S(1)}, u32[]{:S(2)}, u32[]{:S(2)}) collective-permute-start(bf16[128,192]{1,0:T(8,128)(2,1)S(1)} %get-tuple-element.54.a0_ref), channel_id=1, source_target_pairs={{0,32},{4,36},{8,40},{12,44},{16,48},{20,52},{24,56},{28,60},{32,0... | collective-permute-start | bytes 147464 | tf_op jit(solution)/shard_map/ppermute | solution.py:746
  52.3 6.6 %collective-permute-start = (bf16[128,192]{1,0:T(8,128)(2,1)S(1)}, bf16[128,192]{1,0:T(8,128)(2,1)S(1)}, u32[]{:S(2)}, u32[]{:S(2)}) collective-permute-start(bf16[128,192]{1,0:T(8,128)(2,1)S(1)} %get-tuple-element.54.a0_ref), channel_id=1, source_target_pairs={{0,16},{4,20},{8,24},{12,28},{16,0},{20,4},{24,8},{28,12},{32,48},... | collective-permute-start | bytes 147464 | tf_op jit(solution)/shard_map/ppermute | solution.py:746
  60.6 8.2 %collective-permute-start.6 = (bf16[96,128]{1,0:T(8,128)(2,1)S(1)}, bf16[96,128]{1,0:T(8,128)(2,1)S(1)}, u32[]{:S(2)}, u32[]{:S(2)}) collective-permute-start(bf16[96,128]{1,0:T(8,128)(2,1)S(1)} %get-tuple-element.70), channel_id=1, source_target_pairs={{0,48},{4,52},{8,56},{12,60},{16,32},{20,36},{24,40},{28,44},{32,1... | collective-permute-start | bytes 73736 | tf_op jit(solution)/shard_map/ppermute | solution.py:746
  61.9 7.0 %collective-permute-start.7 = (bf16[96,128]{1,0:T(8,128)(2,1)S(1)}, bf16[96,128]{1,0:T(8,128)(2,1)S(1)}, u32[]{:S(2)}, u32[]{:S(2)}) collective-permute-start(bf16[96,128]{1,0:T(8,128)(2,1)S(1)} %get-tuple-element.71), channel_id=1, source_target_pairs={{0,32},{4,36},{8,40},{12,44},{16,48},{20,52},{24,56},{28,60},{32,0... | collective-permute-start | bytes 73736 | tf_op jit(solution)/shard_map/ppermute | solution.py:746
  63.0 5.9 %collective-permute-start.8 = (bf16[96,128]{1,0:T(8,128)(2,1)S(1)}, bf16[96,128]{1,0:T(8,128)(2,1)S(1)}, u32[]{:S(2)}, u32[]{:S(2)}) collective-permute-start(bf16[96,128]{1,0:T(8,128)(2,1)S(1)} %get-tuple-element.72), channel_id=1, source_target_pairs={{0,16},{4,20},{8,24},{12,28},{16,0},{20,4},{24,8},{28,12},{32,48},... | collective-permute-start | bytes 73736 | tf_op jit(solution)/shard_map/ppermute | solution.py:746
  71.9 6.7 %copy-start.6 = (bf16[48,512]{1,0:T(8,128)(2,1)S(1)}, bf16[48,512]{1,0:T(8,128)(2,1)}, u32[]{:S(2)}) copy-start(bf16[48,512]{1,0:T(8,128)(2,1)} %get-tuple-element.75) | copy-start | bytes 147460
  71.9 7.9 %copy-start.5 = (bf16[48,512]{1,0:T(8,128)(2,1)S(1)}, bf16[48,512]{1,0:T(8,128)(2,1)}, u32[]{:S(2)}) copy-start(bf16[48,512]{1,0:T(8,128)(2,1)} %get-tuple-element.76) | copy-start | bytes 147460
  71.9 8.7 %copy-start.4 = (bf16[48,512]{1,0:T(8,128)(2,1)S(1)}, bf16[48,512]{1,0:T(8,128)(2,1)}, u32[]{:S(2)}) copy-start(bf16[48,512]{1,0:T(8,128)(2,1)} %get-tuple-element.77) | copy-start | bytes 147460
  72.0 32.1 %all-to-all-start.1 = ((bf16[128,8,768]{2,1,0:T(8,128)(2,1)}), bf16[128,8,768]{2,1,0:T(8,128)(2,1)S(1)}, u32[]{:S(2)}, u32[]{:S(2)}) async-start(bf16[128,8,768]{2,1,0:T(8,128)(2,1)} %bitcast.13), calls=%async_computation.1 | async-start | bytes 3145728 | tf_op jit(solution)/shard_map/all_to_all | solution.py:770
  78.7 14.7 %collective-permute-start.9 = (bf16[48,512]{1,0:T(8,128)(2,1)S(1)}, bf16[48,512]{1,0:T(8,128)(2,1)S(1)}, u32[]{:S(2)}, u32[]{:S(2)}) collective-permute-start(bf16[48,512]{1,0:T(8,128)(2,1)S(1)} %copy-done.6), channel_id=1, source_target_pairs={{0,4},{4,0},{8,12},{12,8},{16,20},{20,16},{24,28},{28,24},{32,36},... | collective-permute-start | bytes 147464 | tf_op jit(solution)/shard_map/ppermute | solution.py:746
  79.8 13.6 %collective-permute-start.10 = (bf16[48,512]{1,0:T(8,128)(2,1)S(1)}, bf16[48,512]{1,0:T(8,128)(2,1)S(1)}, u32[]{:S(2)}, u32[]{:S(2)}) collective-permute-start(bf16[48,512]{1,0:T(8,128)(2,1)S(1)} %copy-done.5), channel_id=1, source_target_pairs={{0,8},{4,12},{8,0},{12,4},{16,24},{20,28},{24,16},{28,20},{32,40},... | collective-permute-start | bytes 147464 | tf_op jit(solution)/shard_map/ppermute | solution.py:746
  80.6 23.4 %copy-start.2 = (bf16[48,512]{1,0:T(8,128)(2,1)S(1)}, bf16[48,512]{1,0:T(8,128)(2,1)}, u32[]{:S(2)}) copy-start(bf16[48,512]{1,0:T(8,128)(2,1)} %get-tuple-element.74.s0_any) | copy-start | bytes 147460
  80.6 16.9 %collective-permute-start.11 = (bf16[48,512]{1,0:T(8,128)(2,1)S(1)}, bf16[48,512]{1,0:T(8,128)(2,1)S(1)}, u32[]{:S(2)}, u32[]{:S(2)}) collective-permute-start(bf16[48,512]{1,0:T(8,128)(2,1)S(1)} %copy-done.4), channel_id=1, source_target_pairs={{0,12},{4,8},{8,4},{12,0},{16,28},{20,24},{24,20},{28,16},{32,44},... | collective-permute-start | bytes 147464 | tf_op jit(solution)/shard_map/ppermute | solution.py:746

commit v4 on v3

--- a/solution.py
+++ b/solution.py
@@ -161,7 +161,7 @@
 ):
     ff = gate_hbm.shape[1]
     width = HEADS * HD
-    step = 512
+    step = 1024
     chunks = ff // step
     first = started(
         [

time: 115 us -> 115 us (level)
  no operation moved by 1% of the time
where the time goes in v4:
time: 115 us
  Pallas kernels  58.9 us (51%)
  starting transfers between devices  32.4 us (28%)
  waiting for transfers between devices  22.4 us (19%)
    pallas_call x11, Pallas kernels, run(): pl.pallas_call(kernel, out_shape=shapes, in_specs=specs, out_specs=out_sp...  58.9 us
    all_to_all x2, waiting for transfers between devices, exchange(): lax.all_to_all(block.reshape(device_count, SLOTS, slide_width), ('seq', '...  18.3 us
    all_to_all x2, starting transfers between devices, exchange(): lax.all_to_all(block.reshape(device_count, SLOTS, slide_width), ('seq', '...  18.2 us
    ppermute x12, starting transfers between devices, swap(): return lax.ppermute(value, 'seq', [(i, i ^ distance) for i in range(count)])  14.2 us
    ppermute x12, waiting for transfers between devices, swap(): return lax.ppermute(value, 'seq', [(i, i ^ distance) for i in range(count)])  4.19 us
  transfers between devices with their start and end apart: 14, of which 3 were waited for; matrix products, arithmetic and copies ran while one was open for 0% of the time, Pallas kernels for 28%

profile of v4, /device:TPU:1, one launch (start us, length us, event | category | flops | bytes accessed | tf_op | source)
XLA Modules:
  0.0 114.8 jit_solution(4241025057908866758)
XLA Ops:
  0.6 11.6 %shard_map.104 = (bf16[8,128,768]{2,1,0:T(8,128)(2,1)}, bf16[128,768]{1,0:T(8,128)(2,1)}, bf16[128,2048]{1,0:T(8,128)(2,1)}, bf16[128,2048]{1,0:T(8,128)(2,1)}) custom-call(bf16[128,1536]{1,0:T(8,128)(2,1)} %feat_hbm.3, s32[128,128]{1,0:T(8,128)} %bitcast.9, bf16[1536,2048]{1,0:T(8,128)(2,1)} %gate_hbm.3, bf16[1536,2048]{1,0:T(8,128)(2,1)} %up_hbm.3, ...), custom_call_target="tpu_custom_call" | custom-call | tf_op jit(solution)/shard_map/pallas_call | solution.py:66
  12.3 0.0 copy-start.1
  12.3 0.0 copy-start
  12.3 11.5 %all-to-all-start = ((bf16[128,8,768]{2,1,0:T(8,128)(2,1)}), bf16[128,8,768]{2,1,0:T(8,128)(2,1)S(1)}, u32[]{:S(2)}, u32[]{:S(2)}) async-start(bf16[128,8,768]{2,1,0:T(8,128)(2,1)} %bitcast.14), calls=%async_computation | async-start | bytes 3145728 | tf_op jit(solution)/shard_map/all_to_all | solution.py:770
  23.8 0.3 shard_map.109
  24.1 1.1 collective-permute-start.3
  25.3 0.8 collective-permute-start.4
  26.1 0.9 collective-permute-start.5
  27.0 0.9 shard_map.105
  27.9 0.0 copy-start.3
  28.0 9.4 %shard_map.106 = (bf16[2048,1536]{1,0:T(8,128)(2,1)}, bf16[2048,1536]{1,0:T(8,128)(2,1)}) custom-call(bf16[1536,2048]{1,0:T(8,128)(2,1)} %gate_hbm.3, bf16[1536,2048]{1,0:T(8,128)(2,1)} %up_hbm.3, bf16[128,768]{1,0:T(8,128)(2,1)} %get-tuple-element.46._after_hbm.x_hbm), custom_call_target="tpu_custom_call" | custom-call | tf_op jit(solution)/shard_map/pallas_call | solution.py:66
  37.4 11.8 %all-to-all-done = bf16[128,8,768]{2,1,0:T(8,128)(2,1)S(1)} async-done(((bf16[128,8,768]{2,1,0:T(8,128)(2,1)}), bf16[128,8,768]{2,1,0:T(8,128)(2,1)S(1)}, u32[]{:S(2)}, u32[]{:S(2)}) %all-to-all-start) | async-done | bytes 1572896 | tf_op jit(solution)/shard_map/all_to_all | solution.py:770
  49.2 1.9 %shard_map.107 = (bf16[4,512,192]{2,1,0:T(8,128)(2,1)S(1)}, bf16[4,192,512]{2,1,0:T(8,128)(2,1)S(1)}, bf16[128,192]{1,0:T(8,128)(2,1)S(1)}) custom-call(s32[2,16]{1,0:T(2,128)S(1)} %copy-done.3, bf16[1024,768]{1,0:T(8,128)(2,1)S(1)} %bitcast.8, s32[8,1024]{1,0:T(8,128)S(1)} %get-tuple-element.45.tab_ref, bf16[2048,1536]{1,0:T(8,128)(2,1)} %get-tuple-element.47._after_hbm.gate_hbm), custom_call_target="tpu_custom_call" | custom-call | tf_op jit(solution)/shard_map/pallas_call | solution.py:66
  51.1 0.1 collective-permute-start.2
  51.2 1.0 collective-permute-start.1
  52.2 3.2 %collective-permute-start = (bf16[128,192]{1,0:T(8,128)(2,1)S(1)}, bf16[128,192]{1,0:T(8,128)(2,1)S(1)}, u32[]{:S(2)}, u32[]{:S(2)}) collective-permute-start(bf16[128,192]{1,0:T(8,128)(2,1)S(1)} %get-tuple-element.54.a0_ref), channel_id=1, source_target_pairs={{0,16},{4,20},{8,24},{12,28},{16,0},{20,4},{24,8},{28,12},{32,48},... | collective-permute-start | bytes 147464 | tf_op jit(solution)/shard_map/ppermute | solution.py:746
  55.4 3.4 %shard_map.108 = (bf16[4,512,512]{2,1,0:T(8,128)(2,1)S(1)}, bf16[4,512,512]{2,1,0:T(8,128)(2,1)S(1)}, bf16[512,512]{1,0:T(8,128)(2,1)S(1)}, bf16[512,512]{1,0:T(...) custom-call(s32[2,16]{1,0:T(2,128)S(1)} %copy-done.3, ...), custom_call_target="tpu_custom_call" | custom-call | tf_op jit(solution)/shard_map/pallas_call | solution.py:66
  58.8 1.7 %shard_map.110 = (bf16[48,512]{1,0:T(8,128)(2,1)S(1)}, bf16[48,512]{1,0:T(8,128)(2,1)S(1)}, bf16[48,512]{1,0:T(8,128)(2,1)S(1)}, bf16[48,512]{1,0:T(8,128)(2,1)S...) custom-call(s32[2,16]{1,0:T(2,128)S(1)} %copy-done.3, ...), custom_call_target="tpu_custom_call" | custom-call | tf_op jit(solution)/shard_map/pallas_call | solution.py:66
  60.5 1.3 %collective-permute-start.6 = (bf16[96,128]{1,0:T(8,128)(2,1)S(1)}, bf16[96,128]{1,0:T(8,128)(2,1)S(1)}, u32[]{:S(2)}, u32[]{:S(2)}) collective-permute-start(bf16[96,128]{1,0:T(8,128)(2,1)S(1)} %get-tuple-element.70), channel_id=1, source_target_pairs={{0,48},{4,52},{8,56},{12,60},{16,32},{20,36},{24,40},{28,44},{32,1... | collective-permute-start | bytes 73736 | tf_op jit(solution)/shard_map/ppermute | solution.py:746
  61.8 1.1 collective-permute-start.7
  62.9 1.8 %collective-permute-start.8 = (bf16[96,128]{1,0:T(8,128)(2,1)S(1)}, bf16[96,128]{1,0:T(8,128)(2,1)S(1)}, u32[]{:S(2)}, u32[]{:S(2)}) collective-permute-start(bf16[96,128]{1,0:T(8,128)(2,1)S(1)} %get-tuple-element.72), channel_id=1, source_target_pairs={{0,16},{4,20},{8,24},{12,28},{16,0},{20,4},{24,8},{28,12},{32,48},... | collective-permute-start | bytes 73736 | tf_op jit(solution)/shard_map/ppermute | solution.py:746
  64.7 4.0 %shard_map.111 = (bf16[48,512]{1,0:T(8,128)(2,1)}, bf16[48,512]{1,0:T(8,128)(2,1)}, bf16[48,512]{1,0:T(8,128)(2,1)}, bf16[48,512]{1,0:T(8,128)(2,1)}, f32[4,144,512]{2,1,0:T(8,128)S(1)}) custom-call(s32[2,16]{1,0:T(2,128)S(1)} %copy-done.3, bf16[4,512,192]{2,1,0:T(8,128)(2,1)S(1)} %get-tuple-element.48.y_ref, ...), custom_call_target="tpu_custom_call" | custom-call | tf_op jit(solution)/shard_map/pallas_call | solution.py:66
  68.8 3.0 %shard_map.112._after_hbm = bf16[1024,768]{1,0:T(8,128)(2,1)} custom-call(s32[2,16]{1,0:T(2,128)S(1)} %copy-done.3, f32[4,144,512]{2,1,0:T(8,128)S(1)} %get-tuple-element.67.dall_ref, f32[96,128]{1,0:T(8,128)S(1)} %get-tuple-element.68.own_ref, f32[48,128]{1,0:T(8,128)S(1)} %get-tuple-element.69.dq_ref, bf16[96,128]{1,0:T(8,128)(2,1)S(1)} %collective-permute-done.6.r1_ref, ...), custom_call_target="tpu_custom_call" | custom-call | tf_op jit(solution)/shard_map/pallas_call | solution.py:66
  71.8 0.0 copy-start.6
  71.8 6.7 %all-to-all-start.1 = ((bf16[128,8,768]{2,1,0:T(8,128)(2,1)}), bf16[128,8,768]{2,1,0:T(8,128)(2,1)S(1)}, u32[]{:S(2)}, u32[]{:S(2)}) async-start(bf16[128,8,768]{2,1,0:T(8,128)(2,1)} %bitcast.13), calls=%async_computation.1 | async-start | bytes 3145728 | tf_op jit(solution)/shard_map/all_to_all | solution.py:770
  78.5 1.1 collective-permute-start.9
  79.7 0.8 collective-permute-start.10
  80.5 0.9 collective-permute-start.11
  81.4 11.8 %shard_map.113 = (bf16[768,2048]{1,0:T(8,128)(2,1)}, bf16[768,1536]{1,0:T(8,128)(2,1)}, bf16[2304,768]{1,0:T(8,128)(2,1)}) custom-call(bf16[2048,1536]{1,0:T(8,128)(2,1)} %down_hbm.3, bf16[1536,768]{1,0:T(8,128)(2,1)} %proj_hbm.3, bf16[768,2304]{1,0:T(8,128)(2,1)} %qkvw_hbm.3, bf16[1024,768]{1,0:T(8,128)(2,1)} %shard_map.112._after_hbm), custom_call_target="tpu_custom_call" | custom-call | tf_op jit(solution)/shard_map/pallas_call | solution.py:66
  93.3 4.2 %collective-permute-done.11.s3_any = bf16[48,512]{1,0:T(8,128)(2,1)S(1)} collective-permute-done((bf16[48,512]{1,0:T(8,128)(2,1)S(1)}, bf16[48,512]{1,0:T(8,128)(2,1)S(1)}, u32[]{:S(2)}, u32[]{:S(2)}) %collective-permute-start.11) | collective-permute-done | bytes 49184 | tf_op jit(solution)/shard_map/ppermute | solution.py:746
  97.4 6.5 %all-to-all-done.1 = bf16[128,8,768]{2,1,0:T(8,128)(2,1)S(1)} async-done(((bf16[128,8,768]{2,1,0:T(8,128)(2,1)}), bf16[128,8,768]{2,1,0:T(8,128)(2,1)S(1)}, u32[]{:S(2)}, u32[]{:S(2)}) %all-to-all-start.1) | async-done | bytes 1572896 | tf_op jit(solution)/shard_map/all_to_all | solution.py:770
  103.9 10.7 %shard_map.114 = (bf16[128,1536]{1,0:T(8,128)(2,1)}, bf16[192,512]{1,0:T(8,128)(2,1)}) custom-call(bf16[8,128,768]{2,1,0:T(8,128)(2,1)S(1)} %bitcast.7, bf16[48,512]{1,0:T(8,128)(2,1)S(1)} %copy-done.2, bf16[48,512]{1,0:T(8,128)(2,1)S(1)} %collective-permute-done.9.s1_any, bf16[48,512]{1,0:T(8,128)(2,1)S(1)} %collective-permute-done.10.s2_any, ...), custom_call_target="tpu_custom_call" | custom-call | tf_op jit(solution)/shard_map/pallas_call | solution.py:66
  (21 shorter events, 0.0 us)
Async XLA Ops:
  12.3 11.5 %copy-start.1 = (bf16[512,192]{0,1:T(8,128)(2,1)S(1)}, bf16[512,192]{0,1:T(8,128)(2,1)}, u32[]{:S(2)}) copy-start(bf16[512,192]{0,1:T(8,128)(2,1)} %param.17) | copy-start | bytes 589828
  12.3 14.7 %copy-start = (s32[16384]{0:T(1024)S(1)}, s32[16384]{0:T(1024)}, u32[]{:S(2)}) copy-start(s32[16384]{0:T(1024)} %param.15) | copy-start | bytes 196612
  12.3 36.9 %all-to-all-start = ((bf16[128,8,768]{2,1,0:T(8,128)(2,1)}), bf16[128,8,768]{2,1,0:T(8,128)(2,1)S(1)}, u32[]{:S(2)}, u32[]{:S(2)}) async-start(bf16[128,8,768]{2,1,0:T(8,128)(2,1)} %bitcast.14), calls=%async_computation | async-start | bytes 3145728 | tf_op jit(solution)/shard_map/all_to_all | solution.py:770
  24.1 28.0 %collective-permute-start.3 = (bf16[48,512]{1,0:T(8,128)(2,1)S(1)}, bf16[48,512]{1,0:T(8,128)(2,1)S(1)}, u32[]{:S(2)}, u32[]{:S(2)}) collective-permute-start(bf16[48,512]{1,0:T(8,128)(2,1)S(1)} %get-tuple-element.58), channel_id=1, source_target_pairs={{0,4},{4,0},{8,12},{12,8},{16,20},{20,16},{24,28},{28,24},{32,36},... | collective-permute-start | bytes 147464 | tf_op jit(solution)/shard_map/ppermute | solution.py:746
  25.3 33.5 %collective-permute-start.4 = (bf16[48,512]{1,0:T(8,128)(2,1)S(1)}, bf16[48,512]{1,0:T(8,128)(2,1)S(1)}, u32[]{:S(2)}, u32[]{:S(2)}) collective-permute-start(bf16[48,512]{1,0:T(8,128)(2,1)S(1)} %get-tuple-element.59), channel_id=1, source_target_pairs={{0,8},{4,12},{8,0},{12,4},{16,24},{20,28},{24,16},{28,20},{32,40},... | collective-permute-start | bytes 147464 | tf_op jit(solution)/shard_map/ppermute | solution.py:746
  26.1 32.7 %collective-permute-start.5 = (bf16[48,512]{1,0:T(8,128)(2,1)S(1)}, bf16[48,512]{1,0:T(8,128)(2,1)S(1)}, u32[]{:S(2)}, u32[]{:S(2)}) collective-permute-start(bf16[48,512]{1,0:T(8,128)(2,1)S(1)} %get-tuple-element.60), channel_id=1, source_target_pairs={{0,12},{4,8},{8,4},{12,0},{16,28},{20,24},{24,20},{28,16},{32,44},... | collective-permute-start | bytes 147464 | tf_op jit(solution)/shard_map/ppermute | solution.py:746
  27.9 21.2 %copy-start.3 = (s32[2,16]{1,0:T(2,128)S(1)}, s32[2,16]{1,0:T(2,128)}, u32[]{:S(2)}) copy-start(s32[2,16]{1,0:T(2,128)} %shift_ref.9) | copy-start | bytes 388
  51.1 7.7 %collective-permute-start.2 = (bf16[128,192]{1,0:T(8,128)(2,1)S(1)}, bf16[128,192]{1,0:T(8,128)(2,1)S(1)}, u32[]{:S(2)}, u32[]{:S(2)}) collective-permute-start(bf16[128,192]{1,0:T(8,128)(2,1)S(1)} %get-tuple-element.54.a0_ref), channel_id=1, source_target_pairs={{0,48},{4,52},{8,56},{12,60},{16,32},{20,36},{24,40},{28,44},{32,1... | collective-permute-start | bytes 147464 | tf_op jit(solution)/shard_map/ppermute | solution.py:746
  51.2 7.6 %collective-permute-start.1 = (bf16[128,192]{1,0:T(8,128)(2,1)S(1)}, bf16[128,192]{1,0:T(8,128)(2,1)S(1)}, u32[]{:S(2)}, u32[]{:S(2)}) collective-permute-start(bf16[128,192]{1,0:T(8,128)(2,1)S(1)} %get-tuple-element.54.a0_ref), channel_id=1, source_target_pairs={{0,32},{4,36},{8,40},{12,44},{16,48},{20,52},{24,56},{28,60},{32,0... | collective-permute-start | bytes 147464 | tf_op jit(solution)/shard_map/ppermute | solution.py:746
  52.2 6.6 %collective-permute-start = (bf16[128,192]{1,0:T(8,128)(2,1)S(1)}, bf16[128,192]{1,0:T(8,128)(2,1)S(1)}, u32[]{:S(2)}, u32[]{:S(2)}) collective-permute-start(bf16[128,192]{1,0:T(8,128)(2,1)S(1)} %get-tuple-element.54.a0_ref), channel_id=1, source_target_pairs={{0,16},{4,20},{8,24},{12,28},{16,0},{20,4},{24,8},{28,12},{32,48},... | collective-permute-start | bytes 147464 | tf_op jit(solution)/shard_map/ppermute | solution.py:746
  60.5 8.2 %collective-permute-start.6 = (bf16[96,128]{1,0:T(8,128)(2,1)S(1)}, bf16[96,128]{1,0:T(8,128)(2,1)S(1)}, u32[]{:S(2)}, u32[]{:S(2)}) collective-permute-start(bf16[96,128]{1,0:T(8,128)(2,1)S(1)} %get-tuple-element.70), channel_id=1, source_target_pairs={{0,48},{4,52},{8,56},{12,60},{16,32},{20,36},{24,40},{28,44},{32,1... | collective-permute-start | bytes 73736 | tf_op jit(solution)/shard_map/ppermute | solution.py:746
  61.8 7.0 %collective-permute-start.7 = (bf16[96,128]{1,0:T(8,128)(2,1)S(1)}, bf16[96,128]{1,0:T(8,128)(2,1)S(1)}, u32[]{:S(2)}, u32[]{:S(2)}) collective-permute-start(bf16[96,128]{1,0:T(8,128)(2,1)S(1)} %get-tuple-element.71), channel_id=1, source_target_pairs={{0,32},{4,36},{8,40},{12,44},{16,48},{20,52},{24,56},{28,60},{32,0... | collective-permute-start | bytes 73736 | tf_op jit(solution)/shard_map/ppermute | solution.py:746
  62.9 5.8 %collective-permute-start.8 = (bf16[96,128]{1,0:T(8,128)(2,1)S(1)}, bf16[96,128]{1,0:T(8,128)(2,1)S(1)}, u32[]{:S(2)}, u32[]{:S(2)}) collective-permute-start(bf16[96,128]{1,0:T(8,128)(2,1)S(1)} %get-tuple-element.72), channel_id=1, source_target_pairs={{0,16},{4,20},{8,24},{12,28},{16,0},{20,4},{24,8},{28,12},{32,48},... | collective-permute-start | bytes 73736 | tf_op jit(solution)/shard_map/ppermute | solution.py:746
  71.8 6.7 %copy-start.6 = (bf16[48,512]{1,0:T(8,128)(2,1)S(1)}, bf16[48,512]{1,0:T(8,128)(2,1)}, u32[]{:S(2)}) copy-start(bf16[48,512]{1,0:T(8,128)(2,1)} %get-tuple-element.75) | copy-start | bytes 147460
  71.8 7.9 %copy-start.5 = (bf16[48,512]{1,0:T(8,128)(2,1)S(1)}, bf16[48,512]{1,0:T(8,128)(2,1)}, u32[]{:S(2)}) copy-start(bf16[48,512]{1,0:T(8,128)(2,1)} %get-tuple-element.76) | copy-start | bytes 147460
  71.8 8.7 %copy-start.4 = (bf16[48,512]{1,0:T(8,128)(2,1)S(1)}, bf16[48,512]{1,0:T(8,128)(2,1)}, u32[]{:S(2)}) copy-start(bf16[48,512]{1,0:T(8,128)(2,1)} %get-tuple-element.77) | copy-start | bytes 147460
  71.8 32.1 %all-to-all-start.1 = ((bf16[128,8,768]{2,1,0:T(8,128)(2,1)}), bf16[128,8,768]{2,1,0:T(8,128)(2,1)S(1)}, u32[]{:S(2)}, u32[]{:S(2)}) async-start(bf16[128,8,768]{2,1,0:T(8,128)(2,1)} %bitcast.13), calls=%async_computation.1 | async-start | bytes 3145728 | tf_op jit(solution)/shard_map/all_to_all | solution.py:770
  78.5 14.7 %collective-permute-start.9 = (bf16[48,512]{1,0:T(8,128)(2,1)S(1)}, bf16[48,512]{1,0:T(8,128)(2,1)S(1)}, u32[]{:S(2)}, u32[]{:S(2)}) collective-permute-start(bf16[48,512]{1,0:T(8,128)(2,1)S(1)} %copy-done.6), channel_id=1, source_target_pairs={{0,4},{4,0},{8,12},{12,8},{16,20},{20,16},{24,28},{28,24},{32,36},... | collective-permute-start | bytes 147464 | tf_op jit(solution)/shard_map/ppermute | solution.py:746
  79.7 13.6 %collective-permute-start.10 = (bf16[48,512]{1,0:T(8,128)(2,1)S(1)}, bf16[48,512]{1,0:T(8,128)(2,1)S(1)}, u32[]{:S(2)}, u32[]{:S(2)}) collective-permute-start(bf16[48,512]{1,0:T(8,128)(2,1)S(1)} %copy-done.5), channel_id=1, source_target_pairs={{0,8},{4,12},{8,0},{12,4},{16,24},{20,28},{24,16},{28,20},{32,40},... | collective-permute-start | bytes 147464 | tf_op jit(solution)/shard_map/ppermute | solution.py:746
  80.5 23.4 %copy-start.2 = (bf16[48,512]{1,0:T(8,128)(2,1)S(1)}, bf16[48,512]{1,0:T(8,128)(2,1)}, u32[]{:S(2)}) copy-start(bf16[48,512]{1,0:T(8,128)(2,1)} %get-tuple-element.74.s0_any) | copy-start | bytes 147460
  80.5 16.9 %collective-permute-start.11 = (bf16[48,512]{1,0:T(8,128)(2,1)S(1)}, bf16[48,512]{1,0:T(8,128)(2,1)S(1)}, u32[]{:S(2)}, u32[]{:S(2)}) collective-permute-start(bf16[48,512]{1,0:T(8,128)(2,1)S(1)} %copy-done.4), channel_id=1, source_target_pairs={{0,12},{4,8},{8,4},{12,0},{16,28},{20,24},{24,20},{28,16},{32,44},... | collective-permute-start | bytes 147464 | tf_op jit(solution)/shard_map/ppermute | solution.py:746
